TPU v7x, 32 devices: a whole 2x2x4 slice. The times are simulated.
32 devices in a mesh: dp: 4 (over z_hi, core), seq: 4 (over y, x), head: 2 (over z_lo).
Axes of the slice: x: 2, y: 2, z: 4 (z_hi: 2, z_lo: 2; z = z_hi * 2 + z_lo), core: 2. Of those that a mesh axis runs over, the one named last changes fastest.
Arguments:
- hidden_in: bfloat16 [8, 2048, 768], P('dp', ('seq', 'head')), may hold values from -6 to 6
- cotangent: bfloat16 [8, 2048, 768], P('dp', ('seq', 'head')), may hold values from -6 to 6
- lengths: int32 [8], P('dp'), may hold values from 512 to 2048, as said below
- w_qkv: float32 [768, 2304], P(None, 'dp'), may hold values from -0.21875 to 0.21875
- w_out: float32 [768, 768], P(None, 'dp'), may hold values from -1.25 to 1.25
- w_gated: float32 [768, 6144], P(None, 'dp'), may hold values from -0.21875 to 0.21875
- w_down: float32 [3072, 768], P('dp'), may hold values from -0.109375 to 0.109375
- vectors: float32 [11520], P('dp'), may hold values from -0.5 to 1.4, as said below
- mom_qkv: float32 [768, 2304], P(None, 'dp'), may hold values from -80 to 80
- mom_out: float32 [768, 768], P(None, 'dp'), may hold values from -80 to 80
- mom_gated: float32 [768, 6144], P(None, 'dp'), may hold values from -80 to 80
- mom_down: float32 [3072, 768], P('dp'), may hold values from -80 to 80
- vec_first: float32 [11520], P('dp'), may hold values from -40 to 40
- vec_second: float32 [11520], P('dp'), may hold values from 3.2768 to 13.1072
Outputs:
- hidden_out: bfloat16 [8, 2048, 768], P('dp', ('seq', 'head'))
- grad_in: bfloat16 [8, 2048, 768], P('dp', ('seq', 'head'))
- mom_qkv_new: float32 [768, 2304], P(None, 'dp')
- mom_out_new: float32 [768, 768], P(None, 'dp')
- mom_gated_new: float32 [768, 6144], P(None, 'dp')
- mom_down_new: float32 [3072, 768], P('dp')
- w_qkv_new: float32 [768, 2304], P(None, 'dp')
- w_out_new: float32 [768, 768], P(None, 'dp')
- w_gated_new: float32 [768, 6144], P(None, 'dp')
- w_down_new: float32 [3072, 768], P('dp')
- vec_first_new: float32 [11520], P('dp')
- vec_second_new: float32 [11520], P('dp')
- vectors_new: float32 [11520], P('dp')
Inputs may be any that keep to these rules, and one draw needn't show every extreme that they name: `lengths`: in each aligned block of 2 entries, one entry, drawn from the seed, equals 2048. `vectors`: the two norm gains lie between 0.6 and 1.4, every bias between -0.5 and 0.5.
All inputs are finite; a program needn't handle non-finite values.
Results may differ from a plain program's by a relative error of at most 0.028.
Values may be sent and summed in bfloat16 or wider, within the bound.
No kernel may reach another device: no remote copies, remote signals or barrier semaphores. Data moves between devices by JAX's collectives and lax.ppermute only.
A program may use at most 320 MiB of HBM per device.

v0:
```python
import math

import jax
import jax.numpy as jnp
from jax import lax
from jax.sharding import PartitionSpec as P

D = 768
HEADS = 12
HEAD_DIM = 64
FF = 3072
NS_STEPS = 5
STEP = 10


HIGHEST = lax.Precision.HIGHEST
POLY_A = 3.4445
POLY_B = -4.775
POLY_C = 2.0315
MUON_BETA = 0.95
MUON_RATE = 0.3
MUON_DECAY = 0.01
ADAM_BETA_ONE = 0.9
ADAM_BETA_TWO = 0.999
ADAM_RATE = 0.4
ADAM_EPSILON = 1e-08
NORM_EPSILON = 1e-06
MASKED = -1e30


def layer_norm(values, gain, shift):
    centre = values - jnp.mean(values, -1, keepdims=True)
    spread = jnp.mean(centre * centre, -1, keepdims=True)
    return centre * lax.rsqrt(spread + NORM_EPSILON) * gain + shift


def split_vectors(vector, width, hidden):
    base = 4 * width + 2 * hidden
    return (
        vector[:width],
        vector[width : 2 * width],
        vector[2 * width : 3 * width],
        vector[3 * width : 4 * width],
        vector[4 * width : base],
        vector[base : base + width],
        vector[base + width : base + 2 * width],
        vector[base + 2 * width : base + 3 * width],
    )


def head_slopes(first_head, count, heads, length):
    index = (first_head + jnp.arange(count)).astype(jnp.float32)
    return jnp.exp2(-8.0 * (index + 1.0) / heads) * (64.0 / length)


def gelu_product(gated, hidden):
    return jax.nn.gelu(gated[:, :hidden], approximate=False) * gated[:, hidden:]


def score_block(queries, keys_in, query_pos, key_pos, lengths_here, slopes, scale):
    inner = jnp.einsum("bqhe,bkhe->bhqk", queries, keys_in, preferred_element_type=jnp.float32)
    distance = jnp.abs(query_pos[:, None] - key_pos[None, :]).astype(jnp.float32)
    scores = inner * scale - slopes[None, :, None, None] * distance[None, None]
    keep = (key_pos[None, :] < lengths_here[:, None])[:, None, None, :]
    return (scores, keep)


def grad_block(
    queries,
    keys_in,
    values_in,
    grad_out,
    log_total,
    delta,
    query_pos,
    key_pos,
    lengths_here,
    slopes,
    scale,
):
    scores, keep = score_block(queries, keys_in, query_pos, key_pos, lengths_here, slopes, scale)
    weights = jnp.where(keep, jnp.exp(scores - log_total[..., None]), 0.0)
    grad_weights = jnp.einsum(
        "bqhe,bkhe->bhqk", grad_out, values_in, preferred_element_type=jnp.float32
    )
    grad_scores = (weights * (grad_weights - delta[..., None]) * scale).astype(jnp.bfloat16)
    grad_queries = jnp.einsum(
        "bhqk,bkhe->bqhe", grad_scores, keys_in, preferred_element_type=jnp.float32
    )
    grad_keys = jnp.einsum(
        "bhqk,bqhe->bkhe", grad_scores, queries, preferred_element_type=jnp.float32
    )
    grad_values = jnp.einsum(
        "bhqk,bqhe->bkhe",
        weights.astype(jnp.bfloat16),
        grad_out,
        preferred_element_type=jnp.float32,
    )
    return (grad_queries, grad_keys, grad_values)


def make_forward_fold(queries, query_pos, lengths_here, slopes, scale, heads_here, head_dim):

    def fold(carry, piece, start):
        seqs = piece.shape[0]
        count = piece.shape[1]
        step = math.gcd(count, 512)
        blocks = jnp.moveaxis(piece.reshape(seqs, count // step, step, 2, piece.shape[3]), 1, 0)

        def visit(state, item):
            accum, highest, total = state
            block, index = item
            key_pos = index * step + jnp.arange(step)
            keys_in = block[:, :, 0].reshape(seqs, step, heads_here, head_dim)
            values_in = block[:, :, 1].reshape(seqs, step, heads_here, head_dim)
            scores, keep = score_block(
                queries, keys_in, query_pos, key_pos, lengths_here, slopes, scale
            )
            new_high = jnp.maximum(highest, jnp.max(jnp.where(keep, scores, MASKED), -1))
            weights = jnp.where(keep, jnp.exp(scores - new_high[..., None]), 0.0)
            shrink = jnp.exp(highest - new_high)
            total = total * shrink + jnp.sum(weights, -1)
            accum = accum * shrink[..., None] + jnp.einsum(
                "bhqk,bkhe->bhqe",
                weights.astype(jnp.bfloat16),
                values_in,
                preferred_element_type=jnp.float32,
            )
            return ((accum, new_high, total), None)

        state, unused = lax.scan(visit, carry, (blocks, jnp.arange(count // step)))
        return state

    return fold


def local_gram(matrix, wide):
    if wide:
        return jnp.einsum("ik,jk->ij", matrix, matrix, precision=HIGHEST)
    return jnp.einsum("ki,kj->ij", matrix, matrix, precision=HIGHEST)


def apply_poly(current, gram, wide):
    poly = POLY_B * gram + POLY_C * jnp.dot(gram, gram, precision=HIGHEST)
    if wide:
        return POLY_A * current + jnp.dot(poly, current, precision=HIGHEST)
    return POLY_A * current + jnp.dot(current, poly, precision=HIGHEST)


def summed_grams(mats):
    return (
        lax.psum(local_gram(mats[0], True).astype(jnp.bfloat16), "dp").astype(jnp.float32),
        lax.psum(local_gram(mats[1], True).astype(jnp.bfloat16), "dp").astype(jnp.float32),
        lax.psum(local_gram(mats[2], True).astype(jnp.bfloat16), "dp").astype(jnp.float32),
        lax.psum(local_gram(mats[3], False).astype(jnp.bfloat16), "dp").astype(jnp.float32),
    )


def on_device(
    hidden_in,
    cotangent,
    lengths,
    w_qkv,
    w_out,
    w_gated,
    w_down,
    vectors,
    mom_qkv,
    mom_out,
    mom_gated,
    mom_down,
    vec_first,
    vec_second,
):
    seqs, tokens_here, width = hidden_in.shape
    seq_count = lax.axis_size("seq")
    head_count = lax.axis_size("head")
    heads_here = HEADS // head_count
    head_dim = HEAD_DIM
    narrow = width // head_count
    block_rows = tokens_here * head_count
    length = block_rows * seq_count
    scale = 1.0 / math.sqrt(head_dim)
    full_qkv, full_out, full_gated, full_down, full_vectors = (
        lax.all_gather(w_qkv.astype(jnp.bfloat16), "dp", axis=1, tiled=True),
        lax.all_gather(w_out.astype(jnp.bfloat16), "dp", axis=1, tiled=True),
        lax.all_gather(w_gated.astype(jnp.bfloat16), "dp", axis=1, tiled=True),
        lax.all_gather(w_down.astype(jnp.bfloat16), "dp", axis=0, tiled=True),
        lax.all_gather(vectors.astype(jnp.bfloat16), "dp", axis=0, tiled=True),
    )
    hidden = full_down.shape[0]
    value_bias, out_bias, gain_one, shift_one, gated_bias, down_bias, gain_two, shift_two = (
        split_vectors(full_vectors.astype(jnp.float32), width, hidden)
    )
    seq_index = lax.axis_index("seq")
    head_index = lax.axis_index("head")
    token_pos = (seq_index * head_count + head_index) * tokens_here + jnp.arange(tokens_here)
    valid = (token_pos[None, :] < lengths[:, None]).astype(jnp.float32).reshape(seqs * tokens_here)
    rows_in = hidden_in.reshape(seqs * tokens_here, width)
    zero_bias = jnp.zeros((width,), jnp.float32)
    projected = jnp.dot(rows_in, full_qkv, preferred_element_type=jnp.float32) + jnp.concatenate(
        [zero_bias, zero_bias, value_bias]
    )
    projected = projected.astype(jnp.bfloat16).reshape(seqs, tokens_here, 3, width)
    head_rows = lax.all_to_all(projected, "head", split_axis=3, concat_axis=1, tiled=True)
    queries = head_rows[:, :, 0].reshape(seqs, block_rows, heads_here, head_dim)
    pair_local = head_rows[:, :, 1:]
    query_pos = seq_index * block_rows + jnp.arange(block_rows)
    slopes = head_slopes(head_index * heads_here, heads_here, HEADS, length)
    start_state = (
        jnp.zeros((seqs, heads_here, block_rows, head_dim), jnp.float32),
        jnp.full((seqs, heads_here, block_rows), MASKED, jnp.float32),
        jnp.zeros((seqs, heads_here, block_rows), jnp.float32),
    )
    fold = make_forward_fold(queries, query_pos, lengths, slopes, scale, heads_here, head_dim)
    accum, highest, total = fold(
        start_state, lax.all_gather(pair_local, "seq", axis=1, tiled=True), jnp.int32(0)
    )
    attention = accum / total[..., None]
    log_total = highest + jnp.log(total)
    context_heads = (
        jnp.transpose(attention, (0, 2, 1, 3))
        .reshape(seqs, block_rows, narrow)
        .astype(jnp.bfloat16)
    )
    context = lax.all_to_all(
        context_heads, "head", split_axis=1, concat_axis=2, tiled=True
    ).reshape(seqs * tokens_here, width)
    attended = jnp.dot(context, full_out, preferred_element_type=jnp.float32) + out_bias
    residual_one = rows_in.astype(jnp.float32) + attended
    first, norm_one_pull = jax.vjp(layer_norm, residual_one, gain_one, shift_one)
    first_low = first.astype(jnp.bfloat16)
    gated = jnp.dot(first_low, full_gated, preferred_element_type=jnp.float32) + gated_bias

    def glu_local(values):
        return gelu_product(values, hidden)

    mixed_float, glu_pull = jax.vjp(glu_local, gated)
    mixed = mixed_float.astype(jnp.bfloat16)
    ffn = jnp.dot(mixed, full_down, preferred_element_type=jnp.float32) + down_bias
    second, norm_two_pull = jax.vjp(layer_norm, first + ffn, gain_two, shift_two)
    hidden_out = (second * valid[:, None]).astype(jnp.bfloat16).reshape(seqs, tokens_here, width)
    grad_second = cotangent.reshape(seqs * tokens_here, width).astype(jnp.float32) * valid[:, None]
    grad_two, grad_gain_two, grad_shift_two = norm_two_pull(grad_second)
    grad_ffn = grad_two.astype(jnp.bfloat16)
    grad_down_bias = jnp.sum(grad_ffn.astype(jnp.float32), 0)
    grad_down = jnp.einsum("tf,td->fd", mixed, grad_ffn, preferred_element_type=jnp.float32)
    grad_mixed = jnp.einsum("td,fd->tf", grad_ffn, full_down, preferred_element_type=jnp.float32)
    grad_gated = glu_pull(grad_mixed)[0].astype(jnp.bfloat16)
    grad_gated_bias = jnp.sum(grad_gated.astype(jnp.float32), 0)
    grad_gated_weight = jnp.einsum(
        "td,tf->df", first_low, grad_gated, preferred_element_type=jnp.float32
    )
    grad_first = grad_two + jnp.einsum(
        "tf,df->td", grad_gated, full_gated, preferred_element_type=jnp.float32
    )
    grad_one, grad_gain_one, grad_shift_one = norm_one_pull(grad_first)
    grad_att = grad_one.astype(jnp.bfloat16)
    grad_out_bias = jnp.sum(grad_att.astype(jnp.float32), 0)
    grad_out_weight = jnp.einsum("te,td->ed", context, grad_att, preferred_element_type=jnp.float32)
    grad_context = jnp.einsum("td,ed->te", grad_att, full_out, preferred_element_type=jnp.float32)
    grad_context = grad_context.astype(jnp.bfloat16).reshape(seqs, tokens_here, width)
    grad_heads = lax.all_to_all(grad_context, "head", split_axis=2, concat_axis=1, tiled=True)
    grad_out_heads = grad_heads.reshape(seqs, block_rows, heads_here, head_dim)
    delta = jnp.einsum("bqhe,bhqe->bhq", grad_out_heads.astype(jnp.float32), attention)
    pair_all = lax.all_gather(pair_local, "seq", axis=1, tiled=True)
    step = math.gcd(length, 512)
    blocks = jnp.moveaxis(pair_all.reshape(seqs, length // step, step, 2, narrow), 1, 0)

    def visit_keys(grad_q_accum, item):
        block, index = item
        key_pos = index * step + jnp.arange(step)
        keys_in = block[:, :, 0].reshape(seqs, step, heads_here, head_dim)
        values_in = block[:, :, 1].reshape(seqs, step, heads_here, head_dim)
        part_q, part_k, part_v = grad_block(
            queries,
            keys_in,
            values_in,
            grad_out_heads,
            log_total,
            delta,
            query_pos,
            key_pos,
            lengths,
            slopes,
            scale,
        )
        terms = jnp.stack(
            (part_k.reshape(seqs, step, narrow), part_v.reshape(seqs, step, narrow)), 2
        )
        return (grad_q_accum + part_q, terms)

    grad_q_accum, key_terms = lax.scan(
        visit_keys,
        jnp.zeros((seqs, block_rows, heads_here, head_dim), jnp.float32),
        (blocks, jnp.arange(length // step)),
    )
    key_terms = jnp.moveaxis(key_terms, 0, 1).reshape(seqs, length, 2, narrow)
    key_sums = lax.psum_scatter(key_terms, "seq", scatter_dimension=1, tiled=True)
    grad_q_mine = grad_q_accum.reshape(seqs, block_rows, narrow)
    grad_k_mine = key_sums[:, :, 0]
    grad_v_mine = key_sums[:, :, 1]
    grads_heads = jnp.stack(
        (
            grad_q_mine.astype(jnp.bfloat16),
            grad_k_mine.astype(jnp.bfloat16),
            grad_v_mine.astype(jnp.bfloat16),
        ),
        2,
    )
    grads_tokens = lax.all_to_all(grads_heads, "head", split_axis=1, concat_axis=3, tiled=True)
    grad_rows = grads_tokens.reshape(seqs * tokens_here, 3 * width)
    grad_value_bias = jnp.sum(grad_rows[:, 2 * width :].astype(jnp.float32), 0)
    grad_qkv = jnp.einsum("td,tf->df", rows_in, grad_rows, preferred_element_type=jnp.float32)
    grad_input = grad_one + jnp.einsum(
        "tf,df->td", grad_rows, full_qkv, preferred_element_type=jnp.float32
    )
    grad_in = grad_input.astype(jnp.bfloat16).reshape(seqs, tokens_here, width)
    grad_vector = jnp.concatenate(
        [
            grad_value_bias,
            grad_out_bias,
            grad_gain_one,
            grad_shift_one,
            grad_gated_bias,
            grad_down_bias,
            grad_gain_two,
            grad_shift_two,
        ]
    )
    shard_qkv, shard_out, shard_gated, shard_down, shard_vector = (
        lax.psum_scatter(grad_qkv, "dp", scatter_dimension=1, tiled=True),
        lax.psum_scatter(grad_out_weight, "dp", scatter_dimension=1, tiled=True),
        lax.psum_scatter(grad_gated_weight, "dp", scatter_dimension=1, tiled=True),
        lax.psum_scatter(grad_down, "dp", scatter_dimension=0, tiled=True),
        lax.psum_scatter(grad_vector, "dp", scatter_dimension=0, tiled=True),
    )
    summed_qkv, summed_out, summed_gated, summed_down, summed_vector = lax.psum(
        (shard_qkv, shard_out, shard_gated, shard_down, shard_vector), ("seq", "head")
    )
    moments = (
        MUON_BETA * mom_qkv + summed_qkv,
        MUON_BETA * mom_out + summed_out,
        MUON_BETA * mom_gated + summed_gated,
        MUON_BETA * mom_down + summed_down,
    )
    wide_flags = (True, True, True, False)
    grams = summed_grams(moments)
    norms = tuple((jnp.sqrt(jnp.trace(gram)) + 1e-07 for gram in grams))
    currents = tuple((moment / norm_value for moment, norm_value in zip(moments, norms)))
    grams = tuple((gram / (norm_value * norm_value) for gram, norm_value in zip(grams, norms)))
    for turn in range(NS_STEPS):
        if turn > 0:
            grams = summed_grams(currents)
        currents = tuple(
            (
                apply_poly(current, gram, wide)
                for current, gram, wide in zip(currents, grams, wide_flags)
            )
        )
    full_shapes = ((D, 3 * D), (D, D), (D, 2 * FF), (FF, D))
    masters = (w_qkv, w_out, w_gated, w_down)
    new_weights = tuple(
        (
            weight * (1.0 - MUON_RATE * MUON_DECAY)
            - MUON_RATE * 0.2 * math.sqrt(max(shape[0], shape[1])) * current
            for weight, current, shape in zip(masters, currents, full_shapes)
        )
    )
    first_new = ADAM_BETA_ONE * vec_first + (1.0 - ADAM_BETA_ONE) * summed_vector
    second_new = ADAM_BETA_TWO * vec_second + (1.0 - ADAM_BETA_TWO) * summed_vector * summed_vector
    first_hat = first_new / (1.0 - ADAM_BETA_ONE**STEP)
    second_hat = second_new / (1.0 - ADAM_BETA_TWO**STEP)
    vectors_new = vectors - ADAM_RATE * first_hat / (jnp.sqrt(second_hat) + ADAM_EPSILON)
    return (
        hidden_out,
        grad_in,
        moments[0],
        moments[1],
        moments[2],
        moments[3],
        new_weights[0],
        new_weights[1],
        new_weights[2],
        new_weights[3],
        first_new,
        second_new,
        vectors_new,
    )


def solution(mesh):
    in_specs = (
        P("dp", ("seq", "head"), None),
        P("dp", ("seq", "head"), None),
        P("dp"),
        P(None, "dp"),
        P(None, "dp"),
        P(None, "dp"),
        P("dp", None),
        P("dp"),
        P(None, "dp"),
        P(None, "dp"),
        P(None, "dp"),
        P("dp", None),
        P("dp"),
        P("dp"),
    )
    out_specs = (
        P("dp", ("seq", "head"), None),
        P("dp", ("seq", "head"), None),
        P(None, "dp"),
        P(None, "dp"),
        P(None, "dp"),
        P("dp", None),
        P(None, "dp"),
        P(None, "dp"),
        P(None, "dp"),
        P("dp", None),
        P("dp"),
        P("dp"),
        P("dp"),
    )
    return jax.shard_map(
        on_device, mesh=mesh, in_specs=in_specs, out_specs=out_specs, check_vma=False
    )
```

profile of v0, /device:TPU:0, one launch (start us, length us, event | category | flops | bytes accessed | tf_op | source)
XLA Modules:
  0.0 2846.1 jit_solution(11092921052426221092)
XLA Ops:
  11.5 32.7 %all-reduce.3 = bf16[11520]{0:T(1024)(128)(2,1)S(1)} all-reduce(bf16[11520]{0:T(1024)(128)(2,1)S(1)} %dynamic-update-slice), channel_id=1, replica_groups=mesh['dp'=4,'seq'=4,'head'=2] {'dp'}, use_global_device_ids=true, to_apply=%add.3 | all-reduce | flops 11520 | bytes 46080
  44.8 19.1 all-gather.6.cloned.1.call-done
  79.9 32.1 %all_to_all.63 = bf16[2,256,3,768]{1,0,2,3:T(2,128)(2,1)S(1)} all-to-all(bf16[2,256,3,768]{1,0,2,3:T(2,128)(2,1)} %copy.111), channel_id=1, replica_groups=mesh['dp'=4,'seq'=4,'head'=2] {'head'}, dimensions={3} | all-to-all | bytes 4718592 | tf_op jit(solution)/shard_map/all_to_all | solution.py:205
  124.4 62.1 %all-gather.8.cloned.1.call-done = bf16[2,2048,2,384]{3,1,2,0:T(8,128)(2,1)} async-done(((bf16[2,512,2,384]{3,1,2,0:T(8,128)(2,1)}), bf16[2,2048,2,384]{3,1,2,0:T(8,128)(2,1)}) %all-gather.8.cloned.1.call-update) | async-done | bytes 6291472 | tf_op jit(solution)/shard_map/all_gather | solution.py:217
  195.2 71.5 %while.28 = (s32[]{:T(128)}, f32[2,6,512,64]{2,3,1,0:T(8,128)}, f32[2,6,512]{2,1,0:T(8,128)S(1)}, f32[2,6,512]{2,1,0:T(8,128)S(1)}, s32[4]{0:T(128)S(1)}, /*inde...) while((s32[]{:T(128)}, f32[2,6,512,64]{2,3,1,0:T(8,128)}, ...), condition=%wide.region_3.4_spmd.clone, body=%wide.region_0.3_spmd.clone.sunk | while | flops 852918272 | bytes 80361736 | solution.py:131
  275.8 58.4 %all-to-all-done.1 = bf16[2,512,384]{2,0,1:T(2,128)(2,1)S(1)} async-done(((bf16[2,512,384]{2,0,1:T(2,128)(2,1)}), bf16[2,512,384]{2,0,1:T(2,128)(2,1)S(1)}, u32[]{:S(2)}, u32[]{:S(2)}) %all-to-all-start.1) | async-done | bytes 786464 | tf_op jit(solution)/shard_map/all_to_all | solution.py:226
  351.9 14.7 multiply_convert_fusion
  366.5 28.4 all-gather.14.cloned.1.call-done
  457.4 138.7 %while.29 = (s32[]{:T(128)}, f32[2,512,6,64]{1,3,2,0:T(8,128)}, f32[4,2,512,2,384]{4,2,0,3,1:T(8,128)}, bf16[4,2,512,2,384]{2,4,1,3,0:T(8,128)(2,1)}, s32[4]{0:T...) while((s32[]{:T(128)}, f32[2,512,6,64]{1,3,2,0:T(8,128)}, ...), condition=%wide.region_13.14_spmd.clone, body=%wide.region_12.13_spmd.clone.sunk | while | flops 2058094592 | bytes 155538864 | solution.py:293
  627.4 87.8 %reduce-scatter.6.cloned.1.call-done = f32[2,512,2,384]{3,1,2,0:T(8,128)} async-done(((f32[2,2048,2,384]{3,1,2,0:T(8,128)}), f32[2,512,2,384]{3,1,2,0:T(8,128)}) %reduce-scatter.6.cloned.1.call-update) | async-done | bytes 3145744 | tf_op jit(solution)/shard_map/reduce_scatter | solution.py:299
  719.9 43.1 %all_to_all.64 = bf16[2,512,3,384]{3,0,2,1:T(2,128)(2,1)S(1)} all-to-all(bf16[2,512,3,384]{3,0,2,1:T(2,128)(2,1)S(1)} %copy.124), channel_id=1, replica_groups=mesh['dp'=4,'seq'=4,'head'=2] {'head'}, dimensions={1} | all-to-all | bytes 4718592 | tf_op jit(solution)/shard_map/all_to_all | solution.py:311
  778.8 117.8 %reduce-scatter.14.cloned.1.call-done = f32[768,768]{1,0:T(8,128)} async-done(((f32[3072,768]{1,0:T(8,128)}), f32[768,768]{1,0:T(8,128)}) %reduce-scatter.14.cloned.1.call-update) | async-done | bytes 2359312 | tf_op jit(solution)/shard_map/reduce_scatter | solution.py:335
  896.7 243.3 %reduce-scatter.12.cloned.1.call-done = f32[768,1536]{1,0:T(8,128)} async-done(((f32[768,6144]{1,0:T(8,128)}), f32[768,1536]{1,0:T(8,128)}) %reduce-scatter.12.cloned.1.call-update) | async-done | bytes 4718608 | tf_op jit(solution)/shard_map/reduce_scatter | solution.py:334
  1139.9 104.0 %reduce-scatter.8.cloned.1.call-done = f32[768,576]{0,1:T(8,128)} async-done(((f32[768,2304]{0,1:T(8,128)}), f32[768,576]{0,1:T(8,128)}) %reduce-scatter.8.cloned.1.call-update) | async-done | bytes 1769488 | tf_op jit(solution)/shard_map/reduce_scatter | solution.py:332
  1244.1 376.6 %all-reduce.18.cloned.1.call-done = (f32[768,576]{0,1:T(8,128)}, f32[768,192]{0,1:T(8,128)}, f32[768,1536]{1,0:T(8,128)}, f32[768,768]{1,0:T(8,128)}) async-done(((f32[768,576]{0,1:T(8,128)}, f32[768,192]{0,1:T(8,128)}, f32[768,1536]{1,0:T(8,128)}, f32[768,768]{1,0:T(8,128)}), (f32[768,576]{0,1:T(8,128)}, f32[768,192]{0,1:T(8,128)}, f32[768,1536]{1,0:T(8,128)}, ...) | async-done | bytes 9437200 | tf_op jit(solution)/shard_map/psum | solution.py:338
  1656.5 172.0 %all-reduce.28.cloned.1.call-done = (bf16[768,768]{1,0:T(8,128)(2,1)}, bf16[768,768]{1,0:T(8,128)(2,1)}, bf16[768,768]{1,0:T(8,128)(2,1)}, bf16[768,768]{1,0:T(8,128)(2,1)}) async-done(((bf16[768,768]{1,0:T(8,128)(2,1)}, bf16[768,768]{1,0:T(8,128)(2,1)}, bf16[768,768]{1,0:T(8,128)(2,1)}, bf16[768,768]{1,0:T(8,128)(2,1)}), (bf16[768,768]{1,0:T(8,128)(2,1)}, bf16[768,768]{1,0:T(8,128)(2,1)}, ...) | async-done | bytes 4718608 | tf_op jit(solution)/shard_map/psum | solution.py:152
  1843.6 15.2 multiply_add_fusion.4
  1922.1 171.4 %all-reduce.26.cloned.1.call-done = (bf16[768,768]{1,0:T(8,128)(2,1)}, bf16[768,768]{1,0:T(8,128)(2,1)}, bf16[768,768]{1,0:T(8,128)(2,1)}, bf16[768,768]{1,0:T(8,128)(2,1)}) async-done(((bf16[768,768]{1,0:T(8,128)(2,1)}, bf16[768,768]{1,0:T(8,128)(2,1)}, bf16[768,768]{1,0:T(8,128)(2,1)}, bf16[768,768]{1,0:T(8,128)(2,1)}), (bf16[768,768]{1,0:T(8,128)(2,1)}, bf16[768,768]{1,0:T(8,128)(2,1)}, ...) | async-done | bytes 4718608 | tf_op jit(solution)/shard_map/psum | solution.py:152
  2156.6 171.4 %all-reduce.24.cloned.1.call-done = (bf16[768,768]{1,0:T(8,128)(2,1)}, bf16[768,768]{1,0:T(8,128)(2,1)}, bf16[768,768]{1,0:T(8,128)(2,1)}, bf16[768,768]{1,0:T(8,128)(2,1)}) async-done(((bf16[768,768]{1,0:T(8,128)(2,1)}, bf16[768,768]{1,0:T(8,128)(2,1)}, bf16[768,768]{1,0:T(8,128)(2,1)}, bf16[768,768]{1,0:T(8,128)(2,1)}), (bf16[768,768]{1,0:T(8,128)(2,1)}, bf16[768,768]{1,0:T(8,128)(2,1)}, ...) | async-done | bytes 4718608 | tf_op jit(solution)/shard_map/psum | solution.py:152
  2392.6 171.4 %all-reduce.22.cloned.1.call-done = (bf16[768,768]{1,0:T(8,128)(2,1)}, bf16[768,768]{1,0:T(8,128)(2,1)}, bf16[768,768]{1,0:T(8,128)(2,1)}, bf16[768,768]{1,0:T(8,128)(2,1)}) async-done(((bf16[768,768]{1,0:T(8,128)(2,1)}, bf16[768,768]{1,0:T(8,128)(2,1)}, bf16[768,768]{1,0:T(8,128)(2,1)}, bf16[768,768]{1,0:T(8,128)(2,1)}), (bf16[768,768]{1,0:T(8,128)(2,1)}, bf16[768,768]{1,0:T(8,128)(2,1)}, ...) | async-done | bytes 4718608 | tf_op jit(solution)/shard_map/psum | solution.py:152
  2636.8 22.8 all-reduce.4
  2659.7 32.3 %psum.199 = f32[2880]{0:T(1024)S(1)} all-reduce(f32[2880]{0:T(1024)S(1)} %dynamic-slice.2), channel_id=1, replica_groups=mesh['dp'=4,'seq'=4,'head'=2] {'seq','head'}, use_global_device_ids=true, to_apply=%region_56.57 | all-reduce | flops 2880 | bytes 23040 | tf_op jit(solution)/shard_map/psum | solution.py:338
  2698.6 101.8 %all-reduce.20.cloned.1.call-done = (bf16[768,768]{1,0:T(8,128)(2,1)}, bf16[768,768]{1,0:T(8,128)(2,1)}, bf16[768,768]{1,0:T(8,128)(2,1)}, bf16[768,768]{1,0:T(8,128)(2,1)}) async-done(((bf16[768,768]{1,0:T(8,128)(2,1)}, bf16[768,768]{1,0:T(8,128)(2,1)}, bf16[768,768]{1,0:T(8,128)(2,1)}, bf16[768,768]{1,0:T(8,128)(2,1)}), (bf16[768,768]{1,0:T(8,128)(2,1)}, bf16[768,768]{1,0:T(8,128)(2,1)}, ...) | async-done | bytes 4718608 | tf_op jit(solution)/shard_map/psum | solution.py:152
  2815.6 14.4 multiply_subtract_fusion
  (576 shorter events, 727.5 us)
Async XLA Ops:
  7.2 56.7 %all-gather.6.cloned.1.call-start = ((), (), s32[]{:S(2)}) async-start(), calls=%async_computation.9 | async-start | bytes 4423680 | tf_op jit(solution)/shard_map/all_gather | solution.py:185
  9.8 176.7 %all-gather.8.cloned.1.call-start = ((), (), s32[]{:S(2)}) async-start(), calls=%async_computation.10 | async-start | bytes 7864320 | tf_op jit(solution)/shard_map/all_gather | solution.py:217
  118.0 217.2 %all-gather.10.cloned.1.call-start = ((), (), s32[]{:S(2)}) async-start(), calls=%async_computation.11 | async-start | bytes 1474560 | tf_op jit(solution)/shard_map/all_gather | solution.py:186
  118.9 219.4 %all-gather.12.cloned.1.call-start = ((), (), s32[]{:S(2)}) async-start(), calls=%async_computation.12 | async-start | bytes 11796480 | tf_op jit(solution)/shard_map/all_gather | solution.py:187
  270.3 63.8 %all-to-all-start.1 = ((bf16[2,512,384]{2,0,1:T(2,128)(2,1)}), bf16[2,512,384]{2,0,1:T(2,128)(2,1)S(1)}, u32[]{:S(2)}, u32[]{:S(2)}) async-start(bf16[2,512,384]{2,0,1:T(2,128)(2,1)} %copy.116), calls=%async_computation.1 | async-start | bytes 1572864 | tf_op jit(solution)/shard_map/all_to_all | solution.py:226
  273.9 121.1 %all-gather.14.cloned.1.call-start = ((), (), s32[]{:S(2)}) async-start(), calls=%async_computation.13 | async-start | bytes 5898240 | tf_op jit(solution)/shard_map/all_gather | solution.py:188
  337.9 94.0 %copy-start.21 = (f32[512,768]{1,0:T(8,128)}, f32[512,768]{1,0:T(8,128)S(1)}, u32[]{:S(2)}) copy-start(f32[512,768]{1,0:T(8,128)S(1)} %get-tuple-element.442) | copy-start | bytes 4718596
  337.9 94.0 %copy-start.70 = (f32[512]{0:T(512)}, f32[512]{0:T(512)S(1)}, u32[]{:S(2)}) copy-start(f32[512]{0:T(512)S(1)} %broadcast_multiply_fusion.3) | copy-start | bytes 6148
  438.6 15.1 all-to-all-start.2
  442.3 272.9 %reduce-scatter.6.cloned.1.call-start = ((), (), s32[]{:S(2)}) async-start(), calls=%async_computation.14 | async-start | bytes 15728640 | tf_op jit(solution)/shard_map/reduce_scatter | solution.py:299
  596.1 182.7 %reduce-scatter.10.cloned.1.call-start = ((), (), s32[]{:S(2)}) async-start(), calls=%async_computation.16 | async-start | bytes 2949120 | tf_op jit(solution)/shard_map/reduce_scatter | solution.py:333
  599.7 296.9 %reduce-scatter.14.cloned.1.call-start = ((), (), s32[]{:S(2)}) async-start(), calls=%async_computation.18 | async-start | bytes 11796480 | tf_op jit(solution)/shard_map/reduce_scatter | solution.py:335
  609.4 530.5 %reduce-scatter.12.cloned.1.call-start = ((), (), s32[]{:S(2)}) async-start(), calls=%async_computation.17 | async-start | bytes 23592960 | tf_op jit(solution)/shard_map/reduce_scatter | solution.py:334
  625.2 618.7 %reduce-scatter.8.cloned.1.call-start = ((), (), s32[]{:S(2)}) async-start(), calls=%async_computation.15 | async-start | bytes 8847360 | tf_op jit(solution)/shard_map/reduce_scatter | solution.py:332
  778.7 842.0 %all-reduce.18.cloned.1.call-start = ((), (), s32[]{:S(2)}) async-start(), calls=%async_computation.19 | async-start | bytes 18874368 | tf_op jit(solution)/shard_map/psum | solution.py:338
  1243.9 376.9 %copy-start.65 = (f32[768,192]{0,1:T(8,128)S(1)}, f32[768,192]{0,1:T(8,128)}, u32[]{:S(2)}) copy-start(f32[768,192]{0,1:T(8,128)} %param.27) | copy-start | bytes 1769476
  1243.9 381.3 %copy-start.42 = (f32[768,576]{0,1:T(8,128)S(1)}, f32[768,576]{0,1:T(8,128)}, u32[]{:S(2)}) copy-start(f32[768,576]{0,1:T(8,128)} %param.26) | copy-start | bytes 5308420
  1243.9 584.6 %all-reduce.28.cloned.1.call-start = ((), (), s32[]{:S(2)}) async-start(), calls=%async_computation.24 | async-start | bytes 9437184 | tf_op jit(solution)/shard_map/psum | solution.py:152
  1622.1 293.9 %copy-start.33 = (f32[768,192]{0,1:T(8,128)}, f32[768,192]{0,1:T(8,128)S(1)}, u32[]{:S(2)}) copy-start(f32[768,192]{0,1:T(8,128)S(1)} %multiply_add_fusion.17) | copy-start | bytes 1769476
  1633.0 244.6 %copy-start.16 = (f32[768,768]{1,0:T(8,128)}, f32[768,768]{1,0:T(8,128)S(1)}, u32[]{:S(2)}) copy-start(f32[768,768]{1,0:T(8,128)S(1)} %multiply_add_fusion.10) | copy-start | bytes 7077892
  1656.4 437.1 %all-reduce.26.cloned.1.call-start = ((), (), s32[]{:S(2)}) async-start(), calls=%async_computation.23 | async-start | bytes 9437184 | tf_op jit(solution)/shard_map/psum | solution.py:152
  1922.0 406.0 %all-reduce.24.cloned.1.call-start = ((), (), s32[]{:S(2)}) async-start(), calls=%async_computation.22 | async-start | bytes 9437184 | tf_op jit(solution)/shard_map/psum | solution.py:152
  2156.6 407.4 %all-reduce.22.cloned.1.call-start = ((), (), s32[]{:S(2)}) async-start(), calls=%async_computation.21 | async-start | bytes 9437184 | tf_op jit(solution)/shard_map/psum | solution.py:152
  2392.5 407.9 %all-reduce.20.cloned.1.call-start = ((), (), s32[]{:S(2)}) async-start(), calls=%async_computation.20 | async-start | bytes 9437184 | tf_op jit(solution)/shard_map/psum | solution.py:152
  (124 other events, 1095.8 us)
Sparse Core Ops, SparseCore 0:
  10.2 53.6 all-gather.5
  118.2 68.3 all-gather.7
  188.7 24.7 all-gather.9
  215.4 114.8 all-gather.11
  332.3 62.6 all-gather.13
  596.3 118.8 reduce-scatter.5
  718.3 45.7 reduce-scatter.9
  766.8 129.8 reduce-scatter.13
  899.4 240.4 reduce-scatter.11
  1142.3 101.5 reduce-scatter.7
  1246.8 373.9 all-reduce.17
  1656.5 171.9 all-reduce.27
  1922.2 171.3 all-reduce.25
  2156.7 171.3 all-reduce.23
  2392.6 171.3 all-reduce.21
  2627.3 173.0 all-reduce.19
where the time goes:
time: 2850 us
  waiting for transfers between devices  1900 us (67%)
  matrix products  557 us (20%)
  blocking collectives  163 us (6%)
  local copies, waits for them, and re-layouts  109 us (4%)
  other arithmetic  85.5 us (3%)
    psum x5, waiting for transfers between devices, summed_grams(): lax.psum(local_gram(mats[0], True).astype(jnp.bfloat16), 'dp')  788 us
    psum x1, waiting for transfers between devices, on_device(): lax.psum((shard_qkv, shard_out, shard_gated, shard_down, shard_vector), (...  377 us
    reduce_scatter x1, waiting for transfers between devices, on_device(): lax.psum_scatter(grad_gated_weight, 'dp', scatter_dimension=1, tiled=True)  243 us
    reduce_scatter x1, waiting for transfers between devices, on_device(): lax.psum_scatter(grad_down, 'dp', scatter_dimension=0, tiled=True)  118 us
    dot_general x15, matrix products, local_gram(): return jnp.einsum('ik,jk->ij', matrix, matrix, precision=HIGHEST)  115 us
    dot_general x15, matrix products, apply_poly(): return POLY_A * current + jnp.dot(poly, current, precision=HIGHEST)  106 us
    reduce_scatter x1, waiting for transfers between devices, on_device(): lax.psum_scatter(grad_qkv, 'dp', scatter_dimension=1, tiled=True)  104 us
    reduce_scatter x1, waiting for transfers between devices, on_device(): lax.psum_scatter(key_terms, 'seq', scatter_dimension=1, tiled=True)  87.8 us
  transfers between devices with their start and end apart: 18, of which 15 were waited for; matrix products, arithmetic and copies ran while one was open for 6% of the time, Pallas kernels for 0%

commit v1 on v0

v1 whole, which is shorter than its diff:
```python
import functools
import math

import jax
import jax.numpy as jnp
from jax import lax
from jax.experimental import pallas as pl
from jax.experimental.pallas import tpu as pltpu
from jax.sharding import PartitionSpec as P

D = 768
HEADS = 12
HEAD_DIM = 64
FF = 3072
NS_STEPS = 5
STEP = 10

POLY_A = 3.4445
POLY_B = -4.775
POLY_C = 2.0315
MUON_BETA = 0.95
MUON_RATE = 0.3
MUON_DECAY = 0.01
ADAM_BETA_ONE = 0.9
ADAM_BETA_TWO = 0.999
ADAM_RATE = 0.4
ADAM_EPSILON = 1e-08
NORM_EPSILON = 1e-06
MASKED = -1e30

BF = jnp.bfloat16
F32 = jnp.float32
AXES = ("dp", "seq", "head")
VMEM_LIMIT = 60 * 1024 * 1024
NT = (((1,), (1,)), ((), ()))
NN = (((1,), (0,)), ((), ()))
TN = (((0,), (0,)), ((), ()))


def dot(a, b, dims=NN):
    return lax.dot_general(a, b, dims, preferred_element_type=F32)


def split_three(value):
    high = value.astype(BF)
    rest = value - high.astype(F32)
    mid = rest.astype(BF)
    low = (rest - mid.astype(F32)).astype(BF)
    return high.astype(F32), mid.astype(F32), low.astype(F32)


def after(value, *others):
    hbm = pl.BlockSpec(memory_space=pl.ANY)
    return pl.pallas_call(
        lambda *refs: None,
        out_shape=jax.ShapeDtypeStruct(value.shape, value.dtype),
        in_specs=[hbm] * (1 + len(others)),
        out_specs=hbm,
        input_output_aliases={0: 0},
        name="after",
    )(value, *others)


def unfold(ref, block, at, count):
    columns = ref.shape[2] // 2
    return jnp.concatenate([ref[block, :, at : at + count], ref[block, :, columns + at : columns + at + count]], 0)


def fold(ref, block, at, value):
    columns = ref.shape[2] // 2
    half = value.shape[0] // 2
    count = value.shape[1]
    ref[block, :, at : at + count] = value[:half].astype(ref.dtype)
    ref[block, :, columns + at : columns + at + count] = value[half:].astype(ref.dtype)


def sum_split_kernel(places, pairs, with_vector, bits_ref, *refs):
    ins = refs[: 2 * pairs]
    vector = refs[2 * pairs : 2 * pairs + 2]
    outs = refs[len(refs) - 2 * len(places) - with_vector :]
    for place, (pair, low, high, axis, which) in enumerate(places):
        mine = 0 if which is None else bits_ref[which]
        for other, out in enumerate(outs[2 * place : 2 * place + 2]):
            at = mine if other == 0 else 1 - mine
            index = (slice(None),) * axis + (at, Ellipsis, slice(low, high))
            first, second = ins[2 * pair], ins[2 * pair + 1]
            out[...] = (first[index].astype(F32) + second[index].astype(F32)).astype(BF)
    if with_vector:
        outs[-1][...] = vector[0][...] + vector[1][...]


def sum_split(places, bits, pairs, vector=None, waits=()):
    smem = pl.BlockSpec(memory_space=pltpu.SMEM)
    by_half = min(place[3] for place in places) > 0
    arrays = [array for pair in pairs for array in pair]
    shapes = []
    for pair, low, high, axis, which in places:
        shape = pairs[pair][0].shape
        shape = shape[:axis] + shape[axis + 1 : -1] + (high - low,)
        shapes += [jax.ShapeDtypeStruct(shape, BF)] * 2

    def spec(array):
        if by_half:
            return pl.BlockSpec((1,) + array.shape[1:], lambda z: (z,) + (0,) * (len(array.shape) - 1))
        return pl.BlockSpec(memory_space=pltpu.VMEM)

    def whole(array):
        if by_half:
            return pl.BlockSpec(array.shape, lambda z: (0,) * len(array.shape))
        return pl.BlockSpec(memory_space=pltpu.VMEM)

    in_specs = [smem] + [spec(array) for array in arrays]
    out_specs = [spec(shape) for shape in shapes]
    if vector:
        arrays += list(vector)
        in_specs += [whole(vector[0])] * 2
        shapes.append(jax.ShapeDtypeStruct(vector[0].shape, F32))
        out_specs.append(whole(vector[0]))
    return pl.pallas_call(
        functools.partial(sum_split_kernel, places, len(pairs), 1 if vector else 0),
        grid=(2,) if by_half else (),
        out_shape=tuple(shapes),
        in_specs=in_specs + [pl.BlockSpec(memory_space=pl.ANY)] * len(waits),
        out_specs=tuple(out_specs),
        compiler_params=pltpu.CompilerParams(vmem_limit_bytes=VMEM_LIMIT),
        cost_estimate=pl.CostEstimate(
            flops=0, bytes_accessed=sum(3 * 2 * p[0].size for p in pairs), transcendentals=0
        ),
        name="sum_split",
    )(bits, *arrays, *waits)


def join_kernel(places, bits_ref, *refs):
    count = len(places)
    outs = refs[-count:]
    for index, (axis, which) in enumerate(places):
        before = (slice(None),) * axis
        mine = bits_ref[which]
        outs[index][before + (mine,)] = refs[index][before + (0,)]
        outs[index][before + (1 - mine,)] = refs[count + index][before + (0,)]


def join_pairs(places, bits, mine, others, waits=()):
    vmem = pl.BlockSpec(memory_space=pltpu.VMEM)
    smem = pl.BlockSpec(memory_space=pltpu.SMEM)
    shapes = tuple(
        jax.ShapeDtypeStruct(array.shape[:axis] + (2,) + array.shape[axis + 1 :], array.dtype)
        for array, (axis, which) in zip(mine, places)
    )
    return pl.pallas_call(
        functools.partial(join_kernel, places),
        out_shape=shapes,
        in_specs=[smem] + [vmem] * (2 * len(mine)) + [pl.BlockSpec(memory_space=pl.ANY)] * len(waits),
        out_specs=(vmem,) * len(mine),
        compiler_params=pltpu.CompilerParams(vmem_limit_bytes=VMEM_LIMIT),
        cost_estimate=pl.CostEstimate(
            flops=0, bytes_accessed=sum(8 * array.size for array in mine), transcendentals=0
        ),
        name="join_pairs",
    )(bits, *mine, *others, *waits)


def key_features(keys, start, rows, length):
    lane = lax.broadcasted_iota(jnp.int32, (rows, 128), 1)
    pos = start + lax.broadcasted_iota(jnp.int32, (rows, 128), 0)
    low = jnp.bitwise_and(pos, 255)
    feats = jnp.where(lane < 68, (pos - low).astype(F32), jnp.where(lane < 71, low.astype(F32), 1.0))
    feats = jnp.where(lane == 64, jnp.where(pos >= length, MASKED, 0.0), feats)
    wide = jnp.concatenate([keys.astype(F32), jnp.zeros_like(keys, F32)], 1)
    return jnp.where(lane < 64, wide, jnp.where(lane < 77, feats, 0.0))


def query_features(queries, start, rows, slope, log_total):
    lane = lax.broadcasted_iota(jnp.int32, (rows, 128), 1)
    first = lax.broadcasted_iota(jnp.int32, (1, 128), 1)
    pos = (start + lax.broadcasted_iota(jnp.int32, (rows, 128), 0)).astype(F32)
    tilt = jnp.zeros((1, 128), F32)
    for offset, piece in enumerate(split_three(jnp.full((1, 128), slope, F32))):
        tilt = jnp.where((first == 65 + offset) | (first == 68 + offset), -piece, tilt)
    tilt = jnp.broadcast_to(tilt, (rows, 128))
    for offset, piece in enumerate(split_three(pos * slope)):
        tilt = jnp.where(lane == 71 + offset, piece, tilt)
    base = jnp.concatenate([queries.astype(F32) * (1.0 / math.sqrt(HEAD_DIM)), jnp.zeros_like(queries, F32)], 1)
    base = jnp.where(lane == 64, 1.0, base)
    if log_total is not None:
        for offset, piece in enumerate(split_three(log_total)):
            base = jnp.where(lane == 74 + offset, -piece, base)
    return base, tilt


def distances(slope, rows):
    row = lax.broadcasted_iota(jnp.int32, (2 * rows, rows), 0)
    col = lax.broadcasted_iota(jnp.int32, (2 * rows, rows), 1)
    first = jnp.abs(row - col).astype(F32) * slope
    second = jnp.abs(row - col - rows).astype(F32) * slope
    return jnp.zeros_like(first), first, second


def relation(pair, block, mine):
    start = jnp.bitwise_xor(2 * pair, mine)
    other = jnp.bitwise_xor(block, mine)
    behind = jnp.where(start > other, 1, 0)
    before = jnp.where(start + 1 < other, 1, 0)
    return jnp.where(behind + before == 0, 1 + other - start, 0), behind - before


def with_ones(values, count):
    rows = values.shape[0]
    lane = lax.broadcasted_iota(jnp.int32, (rows, 128), 1)
    wide = jnp.concatenate([values.astype(F32), jnp.zeros_like(values, F32)], 1)
    return jnp.where(lane < 64, wide, jnp.where(lane < 64 + count, 1.0, 0.0)).astype(BF)


def attention_forward_kernel(
    rows, q_blocks, k_blocks, heads, info_ref, slope_ref, qkv_ref, out_ref, low_ref, log_ref, q_s, k_s, v_s, t_s, o_s
):
    mine = info_ref[0]
    length = info_ref[1]
    narrow = heads * HEAD_DIM
    for h in range(heads):
        lo = h * HEAD_DIM

        @pl.loop(0, k_blocks)
        def _(r):
            rs = pl.ds(pl.multiple_of(r * rows, rows), rows)
            start = jnp.bitwise_xor(r, mine) * rows
            keys = key_features(unfold(qkv_ref, r, narrow + lo, HEAD_DIM), start, rows, length)
            k_s[h, r] = keys.T.astype(BF)
            v_s[h, rs] = with_ones(unfold(qkv_ref, r, 2 * narrow + lo, HEAD_DIM), 1)

        @pl.loop(0, q_blocks)
        def _(r):
            rs = pl.ds(pl.multiple_of(r * rows, rows), rows)
            start = jnp.bitwise_xor(r, mine) * rows
            queries = unfold(qkv_ref, r, lo, HEAD_DIM)
            base, tilt = query_features(queries, start, rows, slope_ref[h], None)
            q_s[h, 0, rs] = (base - tilt).astype(BF)
            q_s[h, 1, rs] = base.astype(BF)
            q_s[h, 2, rs] = (base + tilt).astype(BF)

        for index, value in enumerate(distances(slope_ref[h], rows)):
            t_s[h, index] = value

    wide = 2 * rows

    def attend(h, pair):
        rs = pl.ds(pl.multiple_of(pair * wide, wide), wide)
        scores = []
        for kb in range(k_blocks):
            index, side = relation(pair, kb, mine)
            scores.append(dot(q_s[h, 1 - side, rs], k_s[h, kb]) - t_s[h, index])
        high = scores[0]
        for s in scores[1:]:
            high = jnp.maximum(high, s)
        high = jnp.max(high, -1, keepdims=True)
        weights = jnp.concatenate([jnp.exp(s - high).astype(BF) for s in scores], 1)
        total = dot(weights, v_s[h])
        norm = total[:, HEAD_DIM : HEAD_DIM + 1]
        return total[:, :HEAD_DIM] / norm, high + jnp.log(norm)

    lane = lax.broadcasted_iota(jnp.int32, (wide, 128), 1)
    if q_blocks == k_blocks:

        @pl.loop(0, q_blocks // 2)
        def _(pair):
            rs = pl.ds(pl.multiple_of(pair * wide, wide), wide)
            results = [attend(h, pair) for h in range(heads)]
            logs = jnp.zeros((wide, 128), F32)
            for h, (value, log) in enumerate(results):
                o_s[h, rs] = value
                logs = jnp.where(lane == h, log, logs)
            log_ref[rs] = logs

    else:
        log_ref[...] = jnp.zeros_like(log_ref)

        @pl.loop(0, heads * q_blocks // 2)
        def _(step):
            h = step // (q_blocks // 2)
            pair = lax.rem(step, q_blocks // 2)
            rs = pl.ds(pl.multiple_of(pair * wide, wide), wide)
            value, log = attend(h, pair)
            o_s[h, rs] = value
            log_ref[rs] = jnp.where(lane == h, log, log_ref[rs])

    for h in range(heads):
        out_ref[:, h * HEAD_DIM : (h + 1) * HEAD_DIM] = o_s[h]
        for r in range(q_blocks):
            fold(low_ref, r, h * HEAD_DIM, o_s[h, r * rows : (r + 1) * rows])


def attention_forward(info, slopes, qkv, rows, q_blocks):
    heads = qkv.shape[2] // (6 * HEAD_DIM)
    k_blocks = qkv.shape[0]
    q_rows = q_blocks * rows
    vmem = pl.BlockSpec(memory_space=pltpu.VMEM)
    smem = pl.BlockSpec(memory_space=pltpu.SMEM)
    return pl.pallas_call(
        functools.partial(attention_forward_kernel, rows, q_blocks, k_blocks, heads),
        out_shape=(
            jax.ShapeDtypeStruct((q_rows, heads * HEAD_DIM), F32),
            jax.ShapeDtypeStruct((q_blocks, rows // 2, 2 * heads * HEAD_DIM), BF),
            jax.ShapeDtypeStruct((q_rows, 128), F32),
        ),
        in_specs=[smem, smem, vmem],
        out_specs=(vmem, vmem, vmem),
        scratch_shapes=[
            pltpu.VMEM((heads, 3, q_rows, 128), BF),
            pltpu.VMEM((heads, k_blocks, 128, rows), BF),
            pltpu.VMEM((heads, k_blocks * rows, 128), BF),
            pltpu.VMEM((heads, 3, 2 * rows, rows), F32),
            pltpu.VMEM((heads, q_rows, HEAD_DIM), F32),
        ],
        compiler_params=pltpu.CompilerParams(vmem_limit_bytes=VMEM_LIMIT),
        cost_estimate=pl.CostEstimate(
            flops=16 * heads * q_rows * k_blocks * rows * HEAD_DIM, bytes_accessed=6_000_000, transcendentals=0
        ),
        name="attention_forward",
    )(info, slopes, qkv)


def attention_backward_kernel(
    rows,
    q_blocks,
    k_blocks,
    heads,
    head,
    info_ref,
    slope_ref,
    qkv_ref,
    att_ref,
    log_ref,
    grad_ref,
    *rest,
):
    out_ref, q_s, qt_s, k_s, v_s, g_s, gt_s, t_s, kt_s, dq_s, dk_s, dv_s = rest[-12:]
    mine = info_ref[0]
    length = info_ref[1]
    narrow = heads * HEAD_DIM
    scale = 1.0 / math.sqrt(HEAD_DIM)
    lo = head * HEAD_DIM
    slope = slope_ref[head]

    @pl.loop(0, k_blocks)
    def _(r):
        rs = pl.ds(pl.multiple_of(r * rows, rows), rows)
        start = jnp.bitwise_xor(r, mine) * rows
        keys = unfold(qkv_ref, r, narrow + lo, HEAD_DIM)
        k_s[rs] = key_features(keys, start, rows, length).astype(BF)
        kt_s[r // 2, lax.rem(r, 2)] = keys.astype(F32).T.astype(BF)
        v_s[rs] = with_ones(unfold(qkv_ref, r, 2 * narrow + lo, HEAD_DIM), 3)

    @pl.loop(0, q_blocks)
    def _(r):
        rs = pl.ds(pl.multiple_of(r * rows, rows), rows)
        start = jnp.bitwise_xor(r, mine) * rows
        queries = unfold(qkv_ref, r, lo, HEAD_DIM)
        log_total = log_ref[rs, head : head + 1]
        base, tilt = query_features(queries, start, rows, slope, log_total)
        q_s[rs] = base.astype(BF)
        base = base.T
        tilt = tilt.T
        qt_s[0, r] = (base - tilt).astype(BF)
        qt_s[1, r] = base.astype(BF)
        qt_s[2, r] = (base + tilt).astype(BF)
        grads = unfold(grad_ref, r, lo, HEAD_DIM).astype(F32)
        delta = jnp.sum(grads * att_ref[rs, lo : lo + HEAD_DIM], -1, keepdims=True)
        lane = lax.broadcasted_iota(jnp.int32, (rows, 128), 1)
        wide = jnp.concatenate([grads, jnp.zeros_like(grads)], 1)
        for offset, piece in zip((64, 65, 66), split_three(delta)):
            wide = jnp.where(lane == offset, -piece, wide)
        g_s[rs] = wide.astype(BF)
        gt_s[r] = wide.T.astype(BF)

    for index, value in enumerate(distances(slope, rows)):
        t_s[index] = value
    dq_s[...] = jnp.zeros_like(dq_s)
    wide = 2 * rows

    @pl.loop(0, k_blocks // 2)
    def _(pair):
        ks = pl.ds(pl.multiple_of(pair * wide, wide), wide)
        keys = k_s[ks]
        values = v_s[ks]
        weights, grad_scores = [], []
        for qb in range(q_blocks):
            index, side = relation(pair, qb, mine)
            w = jnp.exp(dot(keys, qt_s[1 + side, qb]) - t_s[index])
            grad_scores.append((w * dot(values, gt_s[qb])).astype(BF))
            weights.append(w.astype(BF))
        grad_scores = jnp.concatenate(grad_scores, 1)
        dv_s[ks] = dot(jnp.concatenate(weights, 1), g_s[...])[:, :HEAD_DIM]
        dk_s[ks] = dot(grad_scores, q_s[...])[:, :HEAD_DIM]
        dq_s[...] += dot(jnp.concatenate([kt_s[pair, 0], kt_s[pair, 1]], 1), grad_scores)

    for r in range(k_blocks):
        rs = slice(r * rows, (r + 1) * rows)
        if r < q_blocks:
            fold(out_ref, r, 0, dq_s[:, rs].T * scale)
        else:
            fold(out_ref, r, 0, jnp.zeros((rows, HEAD_DIM), F32))
        fold(out_ref, r, HEAD_DIM, dk_s[rs])
        fold(out_ref, r, 2 * HEAD_DIM, dv_s[rs])


def attention_backward(head, info, slopes, qkv, attention, log_total, grads, rows, q_blocks, *others):
    heads = qkv.shape[2] // (6 * HEAD_DIM)
    k_blocks = qkv.shape[0]
    q_rows = q_blocks * rows
    k_rows = k_blocks * rows
    vmem = pl.BlockSpec(memory_space=pltpu.VMEM)
    smem = pl.BlockSpec(memory_space=pltpu.SMEM)
    hbm = pl.BlockSpec(memory_space=pl.ANY)
    return pl.pallas_call(
        functools.partial(attention_backward_kernel, rows, q_blocks, k_blocks, heads, head),
        out_shape=jax.ShapeDtypeStruct((k_blocks, rows // 2, 6 * HEAD_DIM), BF if k_blocks == q_blocks else F32),
        in_specs=[smem, smem, vmem, vmem, vmem, vmem] + [hbm] * len(others),
        out_specs=vmem,
        scratch_shapes=[
            pltpu.VMEM((q_rows, 128), BF),
            pltpu.VMEM((3, q_blocks, 128, rows), BF),
            pltpu.VMEM((k_rows, 128), BF),
            pltpu.VMEM((k_rows, 128), BF),
            pltpu.VMEM((q_rows, 128), BF),
            pltpu.VMEM((q_blocks, 128, rows), BF),
            pltpu.VMEM((3, 2 * rows, rows), F32),
            pltpu.VMEM((k_blocks // 2, 2, HEAD_DIM, rows), BF),
            pltpu.VMEM((HEAD_DIM, q_rows), F32),
            pltpu.VMEM((k_rows, HEAD_DIM), F32),
            pltpu.VMEM((k_rows, HEAD_DIM), F32),
        ],
        compiler_params=pltpu.CompilerParams(vmem_limit_bytes=VMEM_LIMIT),
        cost_estimate=pl.CostEstimate(
            flops=80 * q_rows * k_rows * HEAD_DIM, bytes_accessed=7_000_000, transcendentals=0
        ),
        name="attention_backward",
    )(info, slopes, qkv, attention, log_total, grads, *others)


def split_into(high_ref, low_ref, value):
    high = value.astype(BF)
    high_ref[...] = high
    if low_ref is not None:
        low_ref[...] = (value - high.astype(F32)).astype(BF)


PAIRS = ((0, 0), (1, 1), (2, 2), (0, 1), (0, 2), (1, 2))


def newton_schulz_steps(gram_ref, a0h, a0l, ah, al, bh, bl, qh, ql, q_s, a_s, p_s):
    size = gram_ref.shape[0]
    tile = 256
    count = size // tile
    row = lax.broadcasted_iota(jnp.int32, (size, size), 0)
    col = lax.broadcasted_iota(jnp.int32, (size, size), 1)
    eye = (row == col).astype(F32)
    trace = jnp.sum(jnp.sum(gram_ref[...] * eye, 0, keepdims=True), 1, keepdims=True)
    norm = jnp.sqrt(trace) + 1e-07
    a_s[...] = gram_ref[...] / (norm * norm)
    split_into(a0h, a0l, a_s[...])
    split_into(ah, al, a_s[...])

    def product(target, xh, xl, yh, yl, full, mirror, turned=False):
        for i in range(count):
            ri = slice(i * tile, (i + 1) * tile)
            for k in range(i if mirror else 0, count):
                rk = slice(k * tile, (k + 1) * tile)

                def term(x, y):
                    return dot(x[ri], y[rk], NT) if turned else dot(x[ri], y[:, rk])

                part = term(xh, yh)
                if full:
                    part = part + (term(xh, yl) + term(xl, yh))
                target[ri, rk] = part
                if mirror and k > i:
                    target[rk, ri] = part.T

    def advance(full, gram_full, first=False, last=False):
        product(p_s, ah, al, ah, al, full, True)
        poly = POLY_B * a_s[...] + POLY_C * p_s[...]
        if first:
            q_s[...] = poly + POLY_A * eye
        else:
            split_into(bh, bl if full else None, poly)
            product(p_s, bh, bl, qh, ql, full, False)
            q_s[...] = POLY_A * q_s[...] + p_s[...]
        if not last:
            split_into(qh, ql, q_s[...])
            product(p_s, a0h, a0l, qh, ql, gram_full, False, True)
            split_into(bh, bl, p_s[...])
            product(a_s, qh, ql, bh, bl, gram_full, True)
            split_into(ah, al, a_s[...])

    advance(False, False, first=True)

    @pl.loop(1, NS_STEPS - 2)
    def _(turn):
        advance(False, True)

    advance(True, True)
    advance(True, True, last=True)
    return norm


def ns_scratch(size):
    return [pltpu.VMEM((size, size), BF)] * 8 + [pltpu.VMEM((size, size), F32)] * 3


def newton_schulz_kernel(whole, which_ref, packed_ref, mine_ref, theirs_ref, *rest):
    out_ref, gram_s = rest[-13:-11]
    scratch = rest[-11:]
    tile = packed_ref.shape[3]
    half = tile // 2

    @pl.when(which_ref[0] == whole)
    def _():
        gram_s[...] = dot(mine_ref[...], mine_ref[...], NT) + dot(theirs_ref[...], theirs_ref[...], NT)

    @pl.when(which_ref[0] != whole)
    def _():
        for index, (i, k) in enumerate(PAIRS):
            block = jnp.concatenate([packed_ref[0, index], packed_ref[1, index]], 0)
            gram_s[i * tile : (i + 1) * tile, k * tile : (k + 1) * tile] = block
            if i != k:
                gram_s[k * tile : (k + 1) * tile, i * tile : (i + 1) * tile] = block.T

    norm = newton_schulz_steps(gram_s, *scratch)
    out_ref[...] = (scratch[8][...] / norm).astype(out_ref.dtype)


def newton_schulz(which, packed, mine, theirs, whole, *others):
    size = mine.shape[0]
    vmem = pl.BlockSpec(memory_space=pltpu.VMEM)
    smem = pl.BlockSpec(memory_space=pltpu.SMEM)
    return pl.pallas_call(
        functools.partial(newton_schulz_kernel, whole),
        out_shape=jax.ShapeDtypeStruct((size, size), BF),
        in_specs=[smem] + [vmem] * 3 + [pl.BlockSpec(memory_space=pl.ANY)] * len(others),
        out_specs=vmem,
        scratch_shapes=[pltpu.VMEM((size, size), F32)]
        + [pltpu.VMEM((size, size), BF)] * 8
        + [pltpu.VMEM((size, size), F32)] * 3,
        compiler_params=pltpu.CompilerParams(vmem_limit_bytes=VMEM_LIMIT),
        cost_estimate=pl.CostEstimate(flops=80 * size**3, bytes_accessed=7_000_000, transcendentals=0),
        name="newton_schulz",
    )(which, packed, mine, theirs, *others)


def gram_kernel(gated, out, which_ref, first_ref, second_ref, down_ref, packed_ref):
    tile = packed_ref.shape[3]
    half = tile // 2
    rest = gated - first_ref.shape[1]
    kinds = (
        lambda ri, rk: dot(first_ref[ri], first_ref[rk], NT) + dot(second_ref[ri, :rest], second_ref[rk, :rest], NT),
        lambda ri, rk: dot(down_ref[:, ri], down_ref[:, rk], TN),
        lambda ri, rk: dot(second_ref[ri, rest : rest + out], second_ref[rk, rest : rest + out], NT),
    )
    for index, gram in enumerate(kinds):

        @pl.when(jnp.minimum(which_ref[0], 2) == index)
        def _():
            for place, (i, k) in enumerate(PAIRS):
                block = gram(slice(i * tile, (i + 1) * tile), slice(k * tile, (k + 1) * tile))
                packed_ref[0, place] = block[:half]
                packed_ref[1, place] = block[half:]


def upper_gram(which, first, second, down, gated, out):
    vmem = pl.BlockSpec(memory_space=pltpu.VMEM)
    smem = pl.BlockSpec(memory_space=pltpu.SMEM)
    return pl.pallas_call(
        functools.partial(gram_kernel, gated, out),
        out_shape=jax.ShapeDtypeStruct((2, 6, 128, 256), F32),
        in_specs=[smem] + [vmem] * 3,
        out_specs=vmem,
        compiler_params=pltpu.CompilerParams(vmem_limit_bytes=VMEM_LIMIT),
        cost_estimate=pl.CostEstimate(flops=2 * first.shape[0] ** 2 * gated, bytes_accessed=6_000_000, transcendentals=0),
        name="upper_gram",
    )(which, first, second, down)


def update_kernel(scales, place_ref, *refs):
    halves, others = refs[:4], refs[4:8]
    first_ref, second_ref, down_ref, qkv_ref = refs[8:12]
    w_gated, w_down, w_out, w_qkv = refs[12:16]
    n_gated, n_down, n_out, n_qkv = refs[16:20]
    f_s, sems = refs[20:]
    which = place_ref[0]
    core = place_ref[1]
    half = halves[0].shape[0]
    copies = []
    for index, (mine, theirs) in enumerate(zip(halves, others)):
        m = jnp.bitwise_xor(which, index)
        for k, (ref, at) in enumerate(((mine, core), (theirs, 1 - core))):
            copy = pltpu.make_async_copy(
                ref, f_s.at[m, pl.ds(pl.multiple_of(at * half, half), half)], sems.at[2 * index + k]
            )
            copy.start()
            copies.append(copy)
    for copy in copies:
        copy.wait()
    third = first_ref.shape[1]
    gated = w_gated.shape[1] - third
    out = gated + w_out.shape[0]
    turned = (((0,), (1,)), ((), ()))

    def new(weight, scale, ortho):
        return weight * (1.0 - MUON_RATE * MUON_DECAY) - scale * ortho

    n_gated[:, :third] = new(w_gated[:, :third], scales[0], dot(f_s[0], first_ref[...]))
    n_gated[:, third:] = new(w_gated[:, third:], scales[0], dot(f_s[0], second_ref[:, :gated]))
    n_down[...] = new(w_down[...], scales[1], dot(down_ref[...], f_s[1], NT))
    n_out[...] = new(w_out[...], scales[2], dot(second_ref[:, gated:out], f_s[2], turned))
    n_qkv[...] = new(w_qkv[...], scales[3], dot(qkv_ref[...], f_s[3], turned))


def update(scales, place, halves, others, momenta, weights):
    size = halves[0].shape[1]
    vmem = pl.BlockSpec(memory_space=pltpu.VMEM)
    smem = pl.BlockSpec(memory_space=pltpu.SMEM)
    hbm = pl.BlockSpec(memory_space=pl.ANY)
    return pl.pallas_call(
        functools.partial(update_kernel, scales),
        out_shape=tuple(jax.ShapeDtypeStruct(weight.shape, F32) for weight in weights),
        in_specs=[smem] + [hbm] * 8 + [vmem] * 8,
        out_specs=(vmem,) * 4,
        scratch_shapes=[pltpu.VMEM((4, size, size), BF), pltpu.SemaphoreType.DMA((8,))],
        compiler_params=pltpu.CompilerParams(vmem_limit_bytes=VMEM_LIMIT),
        cost_estimate=pl.CostEstimate(flops=8 * size**3, bytes_accessed=28_000_000, transcendentals=0),
        name="update",
    )(place, *halves, *others, *momenta, *weights)


def project_kernel(
    groups, info_ref, vec_ref, x_ref, own_ref, far_ref, own_two, far_two, out_ref, group_ref, wo_ref, w_s, o_s
):
    core = info_ref[0]
    far = info_ref[1]
    unit = w_s.shape[2]
    seqs = out_ref.shape[0] // groups
    tokens = x_ref.shape[0] // seqs
    for a, refs in enumerate(((own_ref, far_ref), (own_two, far_two))):
        for z, ref in enumerate(refs):
            c = 2 * jnp.bitwise_xor(far, z) + jnp.bitwise_xor(core, a)
            for i in range(3):
                w_s[3 * c + i] = ref[:, i * unit : (i + 1) * unit]
            o_s[c] = ref[:, 3 * unit :]
    for g in range(groups):
        for role in range(3):
            group_ref[g, :, role * unit : (role + 1) * unit] = w_s[role * groups + g]
        part = dot(x_ref[...], group_ref[g])
        bias = jnp.concatenate(
            [jnp.zeros((1, 2 * unit), F32), vec_ref[0:1, g * unit : (g + 1) * unit]], 1
        )
        part = (part + bias).astype(BF)
        for b in range(seqs):
            fold(out_ref, b * groups + g, 0, part[b * tokens : (b + 1) * tokens])
    for c in range(4):
        wo_ref[:, c * unit : (c + 1) * unit] = o_s[c]


def project(info, vec, x, weights, groups, tokens):
    rows, width = x.shape
    unit = width // 4
    vmem = pl.BlockSpec(memory_space=pltpu.VMEM)
    smem = pl.BlockSpec(memory_space=pltpu.SMEM)
    return pl.pallas_call(
        functools.partial(project_kernel, groups),
        out_shape=(
            jax.ShapeDtypeStruct((groups * rows // tokens, tokens // 2, 6 * unit), BF),
            jax.ShapeDtypeStruct((groups, width, 3 * unit), BF),
            jax.ShapeDtypeStruct((width, width), BF),
        ),
        in_specs=[smem] + [vmem] * 6,
        out_specs=(vmem,) * 3,
        scratch_shapes=[pltpu.VMEM((12, width, unit), BF), pltpu.VMEM((4, width, unit), BF)],
        compiler_params=pltpu.CompilerParams(vmem_limit_bytes=VMEM_LIMIT),
        cost_estimate=pl.CostEstimate(
            flops=6 * rows * width * width, bytes_accessed=16_000_000, transcendentals=0
        ),
        name="project",
    )(info, vec, x, *weights)


def norm_back(grad, hat, scale, gain):
    inner = grad * gain
    mean = jnp.mean(inner, -1, keepdims=True)
    along = jnp.mean(inner * hat, -1, keepdims=True)
    return scale * (inner - mean - hat * along)


def feed_forward_kernel(
    groups,
    info_ref,
    vec_ref,
    x_ref,
    ctx_ref,
    cot_ref,
    wo_ref,
    own_ref,
    far_ref,
    own_two,
    far_two,
    out_ref,
    one_ref,
    gctx_ref,
    gvec_ref,
    keep_a,
    send_a,
    keep_b,
    send_b,
    w_s,
    ctx_s,
    hat_one,
    first_s,
    acc_s,
    gate_s,
    up_s,
    stage,
    wo_s,
    ffn_s,
    mixed_s,
    ggate_s,
    gup_s,
    sems,
):
    core = info_ref[0]
    far = info_ref[1]
    start = info_ref[2]
    rows, width = x_ref.shape
    unit = width // groups
    tokens = 2 * ctx_ref.shape[1]
    seqs = rows // tokens
    loads = []
    for a, refs in enumerate(((own_ref, far_ref), (own_two, far_two))):
        for z, ref in enumerate(refs):
            copy = pltpu.make_async_copy(ref.at[:, pl.ds(0, 3 * width)], w_s.at[a, z], sems.at[10 + 2 * a + z])
            copy.start()
            loads.append(copy)
    weights = (w_s.at[0], w_s.at[1])
    grads_a = (keep_a, send_a)
    grads_b = (keep_b, send_b)
    down_at = 2 * width
    part = rows // 2

    def vec(i):
        return vec_ref[i : i + 1, :]

    for b in range(seqs):
        for g in range(groups):
            ctx_s[b * tokens : (b + 1) * tokens, g * unit : (g + 1) * unit] = unfold(ctx_ref, b * groups + g, 0, unit)
    residual = x_ref[...].astype(F32) + dot(ctx_s[...], wo_ref[...]) + vec(1)
    centre = residual - jnp.mean(residual, -1, keepdims=True)
    scale_one = lax.rsqrt(jnp.mean(centre * centre, -1, keepdims=True) + NORM_EPSILON)
    hat = centre * scale_one
    hat_one[...] = hat
    first = hat * vec(2) + vec(3)
    first_s[...] = first.astype(BF)
    acc_s[...] = first + vec(12)
    for copy in loads:
        copy.wait()

    def place(p_rel, s_rel):
        p = jnp.bitwise_xor(core, p_rel)
        s = jnp.bitwise_xor(core, s_rel)
        return p, 2 * p + s, pl.ds(pl.multiple_of(s * width, width), width)

    units = [(p, s) for p in range(2) for s in range(2)]
    half = math.sqrt(0.5)
    for index, (p_rel, s_rel) in enumerate(units):
        p, u, columns = place(p_rel, s_rel)
        down_z = jnp.bitwise_xor(p, far)

        @pl.loop(0, rows // part)
        def _(r):
            rs = pl.ds(pl.multiple_of(r * part, part), part)
            gate = dot(first_s[rs], weights[p_rel][far, :, columns]) + vec_ref[pl.ds(4 + u, 1), :]
            up = dot(first_s[rs], weights[p_rel][1 - far, :, columns]) + vec_ref[pl.ds(8 + u, 1), :]
            cdf = 0.5 + 0.5 * lax.erf(gate * half)
            pdf = jnp.exp(gate * gate * -0.5) * (1.0 / math.sqrt(2.0 * math.pi))
            gelu = gate * cdf
            gate_s[index, rs] = up * (cdf + gate * pdf)
            up_s[index, rs] = gelu
            mixed = (gelu * up).astype(BF)
            mixed_s[index, rs] = mixed
            acc_s[rs] += dot(mixed, weights[s_rel][down_z, :, down_at : down_at + width])

    residual = acc_s[...]
    centre = residual - jnp.mean(residual, -1, keepdims=True)
    scale_two = lax.rsqrt(jnp.mean(centre * centre, -1, keepdims=True) + NORM_EPSILON)
    hat = centre * scale_two
    row = lax.broadcasted_iota(jnp.int32, (rows, 1), 0)
    valid = jnp.zeros((rows, 1), F32)
    for b in range(seqs):
        inside = (row >= b * tokens) & (row < (b + 1) * tokens) & (start + row - b * tokens < info_ref[3 + b])
        valid = jnp.where(inside, 1.0, valid)
    out_ref[...] = ((hat * vec(13) + vec(14)) * valid).astype(BF)
    grad_second = cot_ref[...].astype(F32) * valid
    gvec_ref[13:14, :] = jnp.sum(grad_second * hat, 0, keepdims=True)
    gvec_ref[14:15, :] = jnp.sum(grad_second, 0, keepdims=True)
    gvec_ref[15:16, :] = jnp.zeros((1, width), F32)
    grad_two = norm_back(grad_second, hat, scale_two, vec(13))
    acc_s[...] = grad_two
    grad_ffn = grad_two.astype(BF)
    ffn_s[...] = grad_ffn
    gvec_ref[12:13, :] = jnp.sum(grad_ffn.astype(F32), 0, keepdims=True)

    copies = []

    def write(slot, value, target, z, columns):
        if len(copies) >= 6:
            copies[len(copies) - 6].wait()
        stage[slot] = value.astype(BF)
        copy = pltpu.make_async_copy(stage.at[slot], target.at[z, :, columns], sems.at[slot])
        copy.start()
        copies.append(copy)

    for index, (p_rel, s_rel) in enumerate(units):
        p, u, columns = place(p_rel, s_rel)
        down_z = jnp.bitwise_xor(p, far)
        grad_mixed = dot(ffn_s[...], weights[s_rel][down_z, :, down_at : down_at + width], NT)
        grad_gate = (grad_mixed * gate_s[index]).astype(BF)
        grad_up = (grad_mixed * up_s[index]).astype(BF)
        ggate_s[...] = grad_gate
        gup_s[...] = grad_up
        gvec_ref[pl.ds(4 + u, 1), :] = jnp.sum(grad_gate.astype(F32), 0, keepdims=True)
        gvec_ref[pl.ds(8 + u, 1), :] = jnp.sum(grad_up.astype(F32), 0, keepdims=True)
        acc_s[...] += dot(ggate_s[...], weights[p_rel][far, :, columns], NT)
        acc_s[...] += dot(gup_s[...], weights[p_rel][1 - far, :, columns], NT)
        slot = 3 * (index % 2)
        write(slot, dot(mixed_s[index], ffn_s[...], TN), grads_b[s_rel], down_z, pl.ds(0, width))
        write(slot + 1, dot(first_s[...], ggate_s[...], TN), grads_a[p_rel], far, columns)
        write(slot + 2, dot(first_s[...], gup_s[...], TN), grads_a[p_rel], 1 - far, columns)

    grad_first = acc_s[...]
    hat = hat_one[...]
    gvec_ref[2:3, :] = jnp.sum(grad_first * hat, 0, keepdims=True)
    gvec_ref[3:4, :] = jnp.sum(grad_first, 0, keepdims=True)
    grad_one = norm_back(grad_first, hat, scale_one, vec(2))
    one_ref[...] = grad_one
    grad_att = grad_one.astype(BF)
    gvec_ref[1:2, :] = jnp.sum(grad_att.astype(F32), 0, keepdims=True)
    grad_ctx = dot(grad_att, wo_ref[...], NT).astype(BF)
    gvec_ref[0:1, :] = jnp.sum(grad_ctx.astype(F32), 0, keepdims=True)
    for b in range(seqs):
        for g in range(groups):
            fold(gctx_ref, b * groups + g, 0, grad_ctx[b * tokens : (b + 1) * tokens, g * unit : (g + 1) * unit])
    grad_wo = dot(ctx_s[...], grad_att, TN).astype(BF)
    spare = wo_s.shape[2] - width // 4
    for c in range(4):
        part = grad_wo[:, c * (width // 4) : (c + 1) * (width // 4)]
        wo_s[c] = jnp.concatenate([part, jnp.zeros((width, spare), BF)], 1)
    last = []
    for a in range(2):
        for z in range(2):
            c = 2 * jnp.bitwise_xor(far, z) + jnp.bitwise_xor(core, a)
            copy = pltpu.make_async_copy(
                wo_s.at[c],
                grads_a[a].at[z, :, pl.ds(2 * width, wo_s.shape[2])],
                sems.at[6 + 2 * a + z],
            )
            copy.start()
            last.append(copy)
    for copy in copies[-6:] + last:
        copy.wait()


def feed_forward(info, vec, x, ctx, cot, wo, weights, groups):
    rows, width = x.shape
    vmem = pl.BlockSpec(memory_space=pltpu.VMEM)
    smem = pl.BlockSpec(memory_space=pltpu.SMEM)
    hbm = pl.BlockSpec(memory_space=pl.ANY)
    grads_a = jax.ShapeDtypeStruct((2, width, 2 * width + 256), BF)
    grads_b = jax.ShapeDtypeStruct((2, width, width), BF)
    return pl.pallas_call(
        functools.partial(feed_forward_kernel, groups),
        out_shape=(
            jax.ShapeDtypeStruct((rows, width), BF),
            jax.ShapeDtypeStruct((rows, width), F32),
            jax.ShapeDtypeStruct(ctx.shape, BF),
            jax.ShapeDtypeStruct((16, width), F32),
            grads_a,
            grads_a,
            grads_b,
            grads_b,
        ),
        in_specs=[smem] + [vmem] * 5 + [hbm] * 4,
        out_specs=(vmem,) * 4 + (hbm,) * 4,
        scratch_shapes=[
            pltpu.VMEM((2, 2, width, 3 * width), BF),
            pltpu.VMEM((rows, width), BF),
            pltpu.VMEM((rows, width), F32),
            pltpu.VMEM((rows, width), BF),
            pltpu.VMEM((rows, width), F32),
            pltpu.VMEM((4, rows, width), F32),
            pltpu.VMEM((4, rows, width), F32),
            pltpu.VMEM((6, width, width), BF),
            pltpu.VMEM((4, width, 256), BF),
            pltpu.VMEM((rows, width), BF),
            pltpu.VMEM((4, rows, width), BF),
            pltpu.VMEM((rows, width), BF),
            pltpu.VMEM((rows, width), BF),
            pltpu.SemaphoreType.DMA((14,)),
        ],
        compiler_params=pltpu.CompilerParams(vmem_limit_bytes=VMEM_LIMIT),
        cost_estimate=pl.CostEstimate(
            flops=60 * rows * width * width, bytes_accessed=34_000_000, transcendentals=0
        ),
        name="feed_forward",
    )(info, vec, x, ctx, cot, wo, *weights)


def qkv_grad_kernel(groups, heads, info_ref, x_ref, *refs):
    grad_refs = refs[:heads]
    rows_ref, keep_ref, send_ref, w_s = refs[-4:]
    core = info_ref[0]
    tokens = rows_ref.shape[1]
    seqs = rows_ref.shape[0] // groups
    unit = w_s.shape[2]
    for g in range(groups):
        total = None
        for b in range(seqs):
            owner = b * groups + g
            for role in range(3):
                for h in range(heads):
                    at = role * unit + h * HEAD_DIM
                    rows_ref[owner, :, at : at + HEAD_DIM] = unfold(grad_refs[h], owner, role * HEAD_DIM, HEAD_DIM)
            grads = rows_ref[owner]
            part = dot(x_ref[b * tokens : (b + 1) * tokens, :], grads, TN)
            total = part if total is None else total + part
        for role in range(3):
            w_s[role * groups + g] = total[:, role * unit : (role + 1) * unit].astype(BF)
    for a, ref in enumerate((keep_ref, send_ref)):
        for z in range(2):
            c = 2 * z + jnp.bitwise_xor(core, a)
            for i in range(3):
                at = (3 * z + i) * unit
                ref[:, at : at + unit] = w_s[3 * c + i]


def qkv_grad(info, x, grads, groups, *others):
    rows, width = x.shape
    heads = len(grads)
    unit = heads * HEAD_DIM
    vmem = pl.BlockSpec(memory_space=pltpu.VMEM)
    smem = pl.BlockSpec(memory_space=pltpu.SMEM)
    out = jax.ShapeDtypeStruct((width, 6 * unit), BF)
    return pl.pallas_call(
        functools.partial(qkv_grad_kernel, groups, heads),
        out_shape=(
            jax.ShapeDtypeStruct((grads[0].shape[0], 2 * grads[0].shape[1], 3 * unit), BF),
            out,
            out,
        ),
        in_specs=[smem] + [vmem] * (1 + heads) + [pl.BlockSpec(memory_space=pl.ANY)] * len(others),
        out_specs=(vmem,) * 3,
        scratch_shapes=[pltpu.VMEM((12, width, unit), BF)],
        compiler_params=pltpu.CompilerParams(vmem_limit_bytes=VMEM_LIMIT),
        cost_estimate=pl.CostEstimate(
            flops=6 * rows * width * width, bytes_accessed=9_000_000, transcendentals=0
        ),
        name="qkv_grad",
    )(info, x, *grads, *others)


def input_grad_kernel(groups, one_ref, grad_ref, group_ref, *rest):
    out_ref = rest[-1]
    tokens = grad_ref.shape[1]
    for b in range(grad_ref.shape[0] // groups):
        total = one_ref[b * tokens : (b + 1) * tokens, :]
        for g in range(groups):
            total = total + dot(grad_ref[b * groups + g], group_ref[g], NT)
        out_ref[b * tokens : (b + 1) * tokens, :] = total.astype(BF)


def input_grad(grad_one, grads, group, groups, *others):
    rows, width = grad_one.shape
    vmem = pl.BlockSpec(memory_space=pltpu.VMEM)
    return pl.pallas_call(
        functools.partial(input_grad_kernel, groups),
        out_shape=jax.ShapeDtypeStruct((rows, width), BF),
        in_specs=[vmem] * 3 + [pl.BlockSpec(memory_space=pl.ANY)] * len(others),
        out_specs=vmem,
        compiler_params=pltpu.CompilerParams(vmem_limit_bytes=VMEM_LIMIT),
        cost_estimate=pl.CostEstimate(
            flops=6 * rows * width * width, bytes_accessed=8_000_000, transcendentals=0
        ),
        name="input_grad",
    )(grad_one, grads, group, *others)


def on_device(
    hidden_in,
    cotangent,
    lengths,
    w_qkv,
    w_out,
    w_gated,
    w_down,
    vectors,
    mom_qkv,
    mom_out,
    mom_gated,
    mom_down,
    vec_first,
    vec_second,
):
    seqs, tokens, width = hidden_in.shape
    seq_count = lax.axis_size("seq")
    head_count = lax.axis_size("head")
    n = seq_count * head_count
    bits = n.bit_length() - 1
    length = tokens * n
    d = lax.axis_index("dp")
    seq_index = lax.axis_index("seq")
    head_index = lax.axis_index("head")
    j = seq_index * head_count + head_index
    core = lax.rem(d, 2)
    far = d // 2
    cols = w_qkv.shape[1]
    piece_rows = width // n

    def swap(value, over_dp=0, over_group=0):
        pairs = [
            (a * n + b, (a ^ over_dp) * n + (b ^ over_group)) for a in range(4) for b in range(n)
        ]
        return lax.ppermute(value, AXES, pairs)

    def bit_of(k):
        return lax.rem(j // (2**k), 2)

    def pick(value, index, axis=0):
        return lax.dynamic_index_in_dim(value, index, axis, keepdims=False)

    def join(cur, k, axis):
        other = swap(cur, 0, 2**k)
        first = bit_of(k) == 0
        return jnp.concatenate([jnp.where(first, cur, other), jnp.where(first, other, cur)], axis)

    def gather_group(piece, order):
        cur = piece.reshape((1,) * bits + piece.shape)
        for k in order:
            cur = join(cur, k, bits - 1 - k)
        return cur.reshape((n * piece.shape[0],) + piece.shape[1:])

    head_bits = head_count.bit_length() - 1

    def gather_rows(piece, axis):
        for k in range(head_bits):
            piece = join(piece, k, axis)
        return lax.all_gather(piece, "seq", axis=axis, tiled=True)

    def halve(value, k, axis):
        return pick(value, bit_of(k), axis), pick(value, 1 - bit_of(k), axis)

    def add(kept, got):
        return (kept.astype(F32) + got.astype(F32)).astype(BF)

    def rows_of(value):
        return lax.dynamic_slice_in_dim(value, j * piece_rows, piece_rows, 0)

    piece = swap(jnp.concatenate([rows_of(w_qkv), rows_of(w_out)], 1).astype(BF), 2)
    own_qo = jnp.concatenate([w_qkv, w_out], 1).astype(BF)
    rest_rows = width // seq_count

    def seq_rows(value):
        return lax.dynamic_slice_in_dim(value, seq_index * rest_rows, rest_rows, 0)

    rest = jnp.concatenate([seq_rows(w_gated), seq_rows(w_down)], 1).astype(BF)
    piece = after(piece, rest)
    rest = swap(rest, 2)
    own_rest = jnp.concatenate([w_gated.astype(BF), w_down.astype(BF)], 1)
    own_qo_two = swap(own_qo, 1)
    far_qo = gather_group(piece, range(bits))
    far_qo_two = swap(far_qo, 1)

    vec_low = vectors.astype(BF)
    vec_rel = [vec_low] + [swap(vec_low, k) for k in (1, 2, 3)]
    vec_pair = [
        jnp.where(core == 0, jnp.stack([vec_rel[a], vec_rel[a + 1]]), jnp.stack([vec_rel[a + 1], vec_rel[a]]))
        for a in (0, 2)
    ]
    vec = jnp.concatenate(
        [jnp.where(far == 0, vec_pair[0], vec_pair[1]), jnp.where(far == 0, vec_pair[1], vec_pair[0])]
    ).reshape(-1, width)
    vec = jnp.concatenate([vec.astype(F32), jnp.zeros((1, width), F32)])

    inner = math.gcd(n, seqs * HEADS)
    heads = seqs * HEADS // inner
    groups = inner // seqs
    unit = heads * HEAD_DIM
    me = lax.rem(j, inner)

    def exchange(blocks):
        if n == inner:
            return lax.all_to_all(blocks, ("seq", "head"), 0, 0, tiled=True)
        got = []
        for r in range(inner):
            block = pick(blocks, jnp.bitwise_xor(me, r))
            got.append(block if r == 0 else swap(block, 0, r))
        return jnp.take(jnp.stack(got), jnp.bitwise_xor(jnp.arange(inner), me), axis=0)

    info = jnp.concatenate([jnp.stack([core, far, j * tokens]), lengths]).astype(jnp.int32)
    x = hidden_in.reshape(seqs * tokens, width)
    owned, group_w, w_o = project(info, vec, x, (own_qo, far_qo, own_qo_two, far_qo_two), groups, tokens)
    own_rest_two = swap(own_rest, 1)
    qkv = exchange(owned)
    far_rest = lax.all_gather(after(rest, far_qo), "seq", axis=0, tiled=True)
    if n > inner:
        qkv = jnp.concatenate([qkv] + [swap(qkv, 0, s * inner) for s in range(1, n // inner)], 0)
    first_head = lax.rem(me, groups) * heads
    place = jnp.stack([j - me, pick(lengths, me // groups)]).astype(jnp.int32)
    head_ids = (first_head + jnp.arange(heads)).astype(F32)
    slopes = jnp.exp2(-8.0 * (head_ids + 1.0) / HEADS) * (64.0 / length)
    attention, attention_low, log_total = attention_forward(place, slopes, qkv, tokens, inner)
    context = exchange(attention_low)
    far_rest = after(far_rest, attention_low)
    far_rest_two = swap(far_rest, 1)
    hidden_out, grad_one, grad_context, grad_vec, keep_a, send_a, keep_b, send_b = feed_forward(
        info,
        vec,
        x,
        context,
        cotangent.reshape(seqs * tokens, width),
        w_o,
        (own_rest, far_rest, own_rest_two, far_rest_two),
        groups,
    )
    grad_owned = exchange(grad_context)

    third = keep_a.shape[2] // 2
    orders = [[(k + i) % bits for k in range(bits)] for i in (1, 2, 0)]
    bit_values = jnp.stack([bit_of(k) for k in range(bits)]).astype(jnp.int32)

    def by_bits(value):
        return value.reshape((2,) + (2,) * bits + (piece_rows, value.shape[2]))

    grad_vector = grad_vec[:15].reshape(2, 2, -1)
    vector = pick(grad_vector, core, 1), swap(pick(grad_vector, 1 - core, 1), 1)
    pairs = [(by_bits(keep_a), by_bits(swap(send_a, 1))), (by_bits(keep_b), by_bits(swap(send_b, 1)))]
    spans = [(0, 0, third), (0, third, 2 * third), (1, 0, keep_b.shape[2])]

    def split_step(step, pairs, spans, vector, *waits):
        if step < bits:
            places = [span + (bits - order[step], order[step]) for span, order in zip(spans, orders)]
        else:
            places = [span + (0, None) for span in spans]
        *values, vector = sum_split(places, bit_values, pairs, vector, waits)
        if step == bits:
            return values[::2], values[1::2], vector
        values = [
            value.reshape(value.shape[:place[3]] + (1,) + value.shape[place[3] :])
            for value, place in zip(values, [p for p in places for i in range(2)])
        ]
        got = [swap(value, 0, 2 ** order[step]) for value, order in zip(values[1::2], orders)]
        return list(zip(values[::2], got)), values[1::2], vector

    def backward(head, *others):
        return attention_backward(
            head, place, slopes, qkv, attention, log_total, grad_owned, tokens, inner, *others
        )

    def finish(grads):
        if n > inner:
            total = grads[:inner]
            for s in range(1, n // inner):
                total = total + swap(grads[s * inner : (s + 1) * inner], 0, s * inner)
            grads = total.astype(BF)
        return exchange(grads)

    def own_momentum():
        gated = rows_of(mom_gated)
        out = rows_of(mom_out)
        spare = jnp.zeros((piece_rows, 2 * third - gated.shape[1] - out.shape[1]), F32)
        return gated[:, :third], jnp.concatenate([gated[:, third:], out, spare], 1), rows_of(mom_down)

    old = own_momentum()
    head_rows = []
    waits = []
    for step in range(max(heads, bits)):
        if step < bits:
            pairs, sent, total = split_step(step, pairs, spans, vector, *waits)
            spans = [(i, 0, pair[0].shape[-1]) for i, pair in enumerate(pairs)]
            vector = total, swap(total, 0, 2**step)
            waits = [*sent, total]
        if step < heads:
            if step == heads - 1:
                waits.append(head_rows[0])
            back = backward(step, *waits)
            if step < heads - 1:
                head_rows.append(finish(back))
            waits = [back]
    own_parts, far_parts, total = split_step(bits, pairs, spans, vector, back)
    head_rows.append(finish(after(back, *far_parts)))
    parts = [
        (MUON_BETA * m + value.reshape(m.shape).astype(F32) + swap(other.reshape(m.shape), 2).astype(F32)).astype(BF)
        for m, value, other in zip(old, own_parts, far_parts)
    ]
    summed_vector = pick(total, far) + swap(pick(total, 1 - far), 2)

    def gather_parts(parts, step, *wait):
        others = [swap(part, 0, 2 ** order[step]) for part, order in zip(parts, orders)]
        places = [(bits - 1 - order[step], order[step]) for order in orders]
        return join_pairs(places, bit_values, parts, others, wait)

    shards = [part.reshape((1,) * bits + part.shape) for part in parts]

    grad_rows, keep, send = qkv_grad(info, x, head_rows, groups, *parts, summed_vector)
    shards = gather_parts(shards, 0, send)
    sum_qkv = add(keep, swap(send, 1))
    shards = gather_parts(shards, 1, sum_qkv)
    grad_in = input_grad(grad_one, grad_rows, group_w, groups, sum_qkv, *shards)
    sum_qkv = after(lax.psum_scatter(sum_qkv, "seq", scatter_dimension=0, tiled=True), grad_in)
    for step in range(2, bits):
        shards = gather_parts(shards, step, grad_in)
    shards = [part.reshape(width, part.shape[-1]) for part in shards]
    grad_in = grad_in.reshape(seqs, tokens, width)
    for k in reversed(range(head_bits)):
        kept, send = halve(sum_qkv.reshape(2, sum_qkv.shape[0] // 2, 2 * cols), k, 0)
        sum_qkv = add(kept, swap(send, 0, 2**k))
    old = MUON_BETA * rows_of(mom_qkv)
    near = far == 0
    old = jnp.concatenate([jnp.where(near, old, 0.0), jnp.where(near, 0.0, old)], 1)
    sum_qkv = (sum_qkv.astype(F32) + old).astype(BF)
    far_sum = swap(sum_qkv, 2)

    full_shapes = ((D, 3 * D), (D, D), (D, 2 * FF), (FF, D))
    factors = [MUON_RATE * 0.2 * math.sqrt(max(shape)) for shape in full_shapes]

    stride = seq_count // 4
    which = seq_index // stride
    kind = which.reshape(1).astype(jnp.int32)
    gated_at = w_gated.shape[1] - third
    out_at = gated_at + w_out.shape[1]
    packed = upper_gram(kind, *shards, w_gated.shape[1], w_out.shape[1])
    mine_m = gather_rows(add(sum_qkv, after(far_sum, packed)), 0)
    new_gated = jnp.concatenate([shards[0], shards[1][:, :gated_at]], 1).astype(F32)
    new_out = shards[1][:, gated_at:out_at].astype(F32)
    new_down = shards[2].astype(F32)
    count = len(PAIRS) // head_count
    part = lax.dynamic_slice_in_dim(packed, head_index * count, count, 1)
    part = pick(part, core) + swap(pick(part, 1 - core), 1)
    part = part + after(swap(part, 2), new_gated, new_down)
    theirs_m = swap(mine_m, 1)
    for k in range(head_bits):
        part = join(part, k, 0)
    other_core = swap(part, 1)
    packed = jnp.stack([jnp.where(core == 0, part, other_core), jnp.where(core == 0, other_core, part)])

    low_qkv = jnp.where(near, mine_m[:, :cols], mine_m[:, cols:])
    new_qkv = low_qkv.astype(F32)
    factor = newton_schulz(kind, packed, mine_m, theirs_m, 3, low_qkv)

    half_factor = pick(factor.reshape(2, width // 2, width), core)
    halves = [half_factor] + [swap(half_factor, 0, k * stride * head_count) for k in (1, 2, 3)]
    others = [swap(value, 1) for value in halves]
    new_w_gated, new_w_down, new_w_out, new_w_qkv = update(
        (factors[2], factors[3], factors[1], factors[0]),
        jnp.stack([which, core]).astype(jnp.int32),
        halves,
        others,
        (*shards, low_qkv),
        (w_gated, w_down, w_out.T, w_qkv.T),
    )
    moments = (new_qkv, new_out, new_gated, new_down)
    new_weights = (new_w_qkv.T, new_w_out.T, new_w_gated, new_w_down)
    first_new = ADAM_BETA_ONE * vec_first + (1.0 - ADAM_BETA_ONE) * summed_vector
    second_new = ADAM_BETA_TWO * vec_second + (1.0 - ADAM_BETA_TWO) * summed_vector * summed_vector
    first_hat = first_new / (1.0 - ADAM_BETA_ONE**STEP)
    second_hat = second_new / (1.0 - ADAM_BETA_TWO**STEP)
    vectors_new = vectors - ADAM_RATE * first_hat / (jnp.sqrt(second_hat) + ADAM_EPSILON)
    hidden_out = hidden_out.reshape(seqs, tokens, width)
    return (hidden_out, grad_in) + moments + new_weights + (first_new, second_new, vectors_new)


def solution(mesh):
    tokens = P("dp", ("seq", "head"), None)
    wide = P(None, "dp")
    tall = P("dp", None)
    flat = P("dp")
    in_specs = (tokens, tokens, flat) + (wide, wide, wide, tall, flat) + (wide, wide, wide, tall, flat, flat)
    out_specs = (tokens, tokens) + (wide, wide, wide, tall) * 2 + (flat, flat, flat)
    return jax.shard_map(on_device, mesh=mesh, in_specs=in_specs, out_specs=out_specs, check_vma=False)
```

time: 2850 us -> 602 us (0.21)
  waiting for transfers between devices: 1900 us -> 164 us
  matrix products: 557 us -> 0 us
  Pallas kernels: 0 us -> 248 us
  blocking collectives: 163 us -> 0 us
  starting transfers between devices: 8.62 us -> 91.4 us
  local copies, waits for them, and re-layouts: 109 us -> 34.5 us
  other arithmetic: 85.5 us -> 42.4 us
    psum x6 -> x0, waiting for transfers between devices: 1160 us -> none  [the longest x5 788 us: summed_grams(): lax.psum(local_gram(mats[0], True).astype(jnp.bfloat16), 'dp')]
    dot_general x100 -> x0, matrix products: 557 us -> none  [the longest x15 115 us: local_gram(): return jnp.einsum('ik,jk->ij', matrix, matrix, precision=HIGHEST)]
    reduce_scatter x5 -> x1, waiting for transfers between devices: 553 us -> 0.34 us  [on_device(): lax.psum_scatter(sum_qkv, 'seq', scatter_dimension=0, tiled=True)]
    pallas_call x0 -> x25, Pallas kernels: none -> 248 us  [the longest x3 64.6 us: attention_backward(): pl.pallas_call(functools.partial(attention_backward_kernel, rows, q_block...]
    ppermute x0 -> x56, waiting for transfers between devices: none -> 125 us  [swap(): return lax.ppermute(value, AXES, pairs)]
    all_gather x5 -> x2, waiting for transfers between devices: 110 us -> 7.28 us  [the longest x1 7.28 us: gather_rows(): return lax.all_gather(piece, 'seq', axis=axis, tiled=True)]
    all_to_all x2 -> x0, blocking collectives: 75.2 us -> none  [the longest x1 43.1 us: on_device(): lax.all_to_all(grads_heads, 'head', split_axis=1, concat_axis=3, tiled=True)]
    ppermute x0 -> x56, starting transfers between devices: none -> 63.4 us  [swap(): return lax.ppermute(value, AXES, pairs)]
  transfers between devices with their start and end apart: 18 -> 65, of which waited for: 15 -> 29; matrix products, arithmetic and copies ran while one was open for 6% -> 9% of each run, Pallas kernels for 0% -> 25%
where the time goes in v1:
time: 602 us; the launch traced here: 596 us
  Pallas kernels  248 us (41%)
  waiting for transfers between devices  164 us (27%)
  starting transfers between devices  91.4 us (15%)
  other arithmetic  42.4 us (7%)
  local copies, waits for them, and re-layouts  34.5 us (6%)
  between operations  15 us (2%)
    ppermute x56, waiting for transfers between devices, swap(): return lax.ppermute(value, AXES, pairs)  125 us
    pallas_call x3, Pallas kernels, attention_backward(): pl.pallas_call(functools.partial(attention_backward_kernel, rows, q_block...  64.6 us
    ppermute x56, starting transfers between devices, swap(): return lax.ppermute(value, AXES, pairs)  63.4 us
    pallas_call x1, Pallas kernels, feed_forward(): pl.pallas_call(functools.partial(feed_forward_kernel, groups), out_shape=...  42.1 us
    pallas_call x1, Pallas kernels, attention_forward(): pl.pallas_call(functools.partial(attention_forward_kernel, rows, q_blocks...  35.1 us
    pallas_call x1, Pallas kernels, newton_schulz(): pl.pallas_call(functools.partial(newton_schulz_kernel, whole), out_shape=...  34.6 us
    all_to_all x6, waiting for transfers between devices, exchange(): return lax.all_to_all(blocks, ('seq', 'head'), 0, 0, tiled=True)  31.7 us
    all_to_all x6, starting transfers between devices, exchange(): return lax.all_to_all(blocks, ('seq', 'head'), 0, 0, tiled=True)  27.3 us
  transfers between devices with their start and end apart: 65, of which 29 were waited for; matrix products, arithmetic and copies ran while one was open for 9% of the time, Pallas kernels for 25%

profile of v1, /device:TPU:0, one launch (start us, length us, event | category | flops | bytes accessed | tf_op | source)
XLA Modules:
  0.0 595.8 jit_solution(5256966943249280739)
XLA Ops:
  31.1 5.8 collective-permute-done.5
  64.6 7.8 %project.1 = (bf16[8,128,1152]{2,1,0:T(8,128)(2,1)}, bf16[4,768,576]{2,1,0:T(8,128)(2,1)}, bf16[768,768]{1,0:T(8,128)(2,1)}) custom-call(s32[5]{0:T(128)} %pad_add_fusion.info_ref, f32[16,768]{1,0:T(8,128)} %pad_convert_fusion.vec_ref, bf16[512,768]{1,0:T(8,128)(2,1)} %bitcast.135, bf16[768,768]{1,0:T(8,128)(2,1)} %pad_maximum_fusion.2.own_ref, ...), custom_call_target="tpu_custom_call" | custom-call | flops 1811939328 | bytes 16000000 | tf_op jit(solution)/shard_map/project/pallas_call | solution.py:668
  77.0 11.6 %collective-permute-done.9.refs_0_ = bf16[192,2304]{1,0:T(8,128)(2,1)} collective-permute-done((bf16[192,2304]{1,0:T(8,128)(2,1)}, bf16[192,2304]{1,0:T(8,128)(2,1)}, u32[]{:S(2)}, u32[]{:S(2)}) %collective-permute-start.9) | collective-permute-done | bytes 884768 | tf_op jit(solution)/shard_map/ppermute | solution.py:1028
  96.3 18.5 %all-to-all-done.qkv_ref = bf16[8,128,1152]{2,1,0:T(8,128)(2,1)} async-done(((bf16[8,128,1152]{2,1,0:T(8,128)(2,1)}), bf16[8,128,1152]{2,1,0:T(8,128)(2,1)}, u32[]{:S(2)}, u32[]{:S(2)}) %all-to-all-start) | async-done | bytes 2359328 | tf_op jit(solution)/shard_map/all_to_all | solution.py:1097
  114.8 35.1 %attention_forward.1 = (f32[2048,192]{1,0:T(8,128)}, bf16[8,128,384]{2,1,0:T(8,128)(2,1)}, f32[2048,128]{1,0:T(8,128)}) custom-call(s32[2]{0:T(128)} %pad_add_fusion.1.info_ref, f32[3]{0:T(128)} %exponential_multiply_fusion.slope_ref, bf16[8,128,1152]{2,1,0:T(8,128)(2,1)} %all-to-all-done.qkv_ref), custom_call_target="tpu_custom_call" | custom-call | flops 12884901888 | bytes 6000000 | tf_op jit(solution)/shard_map/attention_forward/pallas_call | solution.py:298
  149.9 5.6 all-to-all-start.1
  155.5 13.2 %all-to-all-done.1.ctx_ref = bf16[8,128,384]{2,1,0:T(8,128)(2,1)S(1)} async-done(((bf16[8,128,384]{2,1,0:T(8,128)(2,1)}), bf16[8,128,384]{2,1,0:T(8,128)(2,1)S(1)}, u32[]{:S(2)}, u32[]{:S(2)}) %all-to-all-start.1) | async-done | bytes 786464 | tf_op jit(solution)/shard_map/all_to_all | solution.py:1097
  169.6 42.1 %feed_forward.1 = (bf16[512,768]{1,0:T(8,128)(2,1)}, f32[512,768]{1,0:T(8,128)}, bf16[8,128,384]{2,1,0:T(8,128)(2,1)}, f32[16,768]{1,0:T(8,128)}, bf16[2,768,179...) custom-call(s32[5]{0:T(128)} %pad_add_fusion.info_ref, ...), custom_call_target="tpu_custom_call" | custom-call | flops 18119393280 | bytes 34000000 | tf_op jit(solution)/shard_map/feed_forward/pallas_call | solution.py:876
  224.5 8.4 %sum_split.4 = (bf16[2,2,2,96,896]{4,3,2,1,0:T(8,128)(2,1)}, bf16[2,2,2,96,896]{4,3,2,1,0:T(8,128)(2,1)}, bf16[2,2,2,96,896]{4,3,2,1,0:T(8,128)(2,1)}, bf16[2,2,...) custom-call(s32[3]{0:T(128)} %pad_add_fusion.2.bits_ref, ...), custom_call_target="tpu_custom_call" | custom-call | bytes 23592960 | tf_op jit(solution)/shard_map/sum_split/pallas_call | solution.py:119
  236.4 21.2 %attention_backward.3.refs_8_ = bf16[8,128,384]{2,1,0:T(8,128)(2,1)} custom-call(s32[2]{0:T(128)} %pad_add_fusion.1.info_ref, f32[3]{0:T(128)} %exponential_multiply_fusion.slope_ref, bf16[8,128,1152]{2,1,0:T(8,128)(2,1)} %all-to-all-done.qkv_ref, f32[2048,192]{1,0:T(8,128)} %get-tuple-element.76.att_ref, f32[2048,128]{1,0:T(8,128)} %get-tuple-element.77.log_ref, ...), custom_call_target="tpu_custom_call" | custom-call | flops 21474836480 | bytes 7000000 | tf_op jit(solution)/shard_map/attention_backward/pallas_call | solution.py:414
  281.0 22.3 %attention_backward.4.refs_8_ = bf16[8,128,384]{2,1,0:T(8,128)(2,1)} custom-call(s32[2]{0:T(128)} %pad_add_fusion.1.info_ref, f32[3]{0:T(128)} %exponential_multiply_fusion.slope_ref, bf16[8,128,1152]{2,1,0:T(8,128)(2,1)} %all-to-all-done.qkv_ref, f32[2048,192]{1,0:T(8,128)} %get-tuple-element.76.att_ref, f32[2048,128]{1,0:T(8,128)} %get-tuple-element.77.log_ref, ...), custom_call_target="tpu_custom_call" | custom-call | flops 21474836480 | bytes 7000000 | tf_op jit(solution)/shard_map/attention_backward/pallas_call | solution.py:414
  316.6 21.2 %attention_backward.5.refs_8_.refs_0_ = bf16[8,128,384]{2,1,0:T(8,128)(2,1)} custom-call(s32[2]{0:T(128)} %pad_add_fusion.1.info_ref, f32[3]{0:T(128)} %exponential_multiply_fusion.slope_ref, bf16[8,128,1152]{2,1,0:T(8,128)(2,1)} %all-to-all-done.qkv_ref, f32[2048,192]{1,0:T(8,128)} %get-tuple-element.76.att_ref, f32[2048,128]{1,0:T(8,128)} %get-tuple-element.77.log_ref, ...), custom_call_target="tpu_custom_call" | custom-call | flops 21474836480 | bytes 7000000 | tf_op jit(solution)/shard_map/attention_backward/pallas_call | solution.py:414
  355.9 6.9 %collective-permute-done.29 = bf16[96,768]{1,0:T(8,128)(2,1)S(1)} collective-permute-done((bf16[96,768]{1,0:T(8,128)(2,1)}, bf16[96,768]{1,0:T(8,128)(2,1)S(1)}, u32[]{:S(2)}, u32[]{:S(2)}) %collective-permute-start.29) | collective-permute-done | bytes 147488 | tf_op jit(solution)/shard_map/ppermute | solution.py:1028
  369.1 9.5 %qkv_grad.1 = (bf16[8,256,576]{2,1,0:T(8,128)(2,1)}, bf16[768,1152]{1,0:T(8,128)(2,1)}, bf16[768,1152]{1,0:T(8,128)(2,1)}) custom-call(s32[5]{0:T(128)} %pad_add_fusion.info_ref, bf16[512,768]{1,0:T(8,128)(2,1)} %bitcast.137, bf16[8,128,384]{2,1,0:T(8,128)(2,1)} %all-to-all-done.3.rest_4_.refs_0_, bf16[8,128,384]{2,1,0:T(8,128)(2,1)} %copy-done.18, ...), custom_call_target="tpu_custom_call" | custom-call | flops 1811939328 | bytes 9000000 | tf_op jit(solution)/shard_map/qkv_grad/pallas_call | solution.py:949
  389.7 5.3 collective-permute-done.34.refs_5_
  401.8 8.4 %collective-permute-done.37.refs_5_ = bf16[1,1,2,96,768]{4,3,2,1,0:T(8,128)(2,1)S(1)} collective-permute-done((bf16[1,1,2,96,768]{4,3,2,1,0:T(8,128)(2,1)}, bf16[1,1,2,96,768]{4,3,2,1,0:T(8,128)(2,1)S(1)}, u32[]{:S(2)}, u32[]{:S(2)}) %collective-permute-start.37) | collective-permute-done | bytes 294944 | tf_op jit(solution)/shard_map/ppermute | solution.py:1028
  418.8 6.9 %input_grad.1.refs_1_.refs_6_ = bf16[512,768]{1,0:T(8,128)(2,1)} custom-call(f32[512,768]{1,0:T(8,128)} %get-tuple-element.75.one_ref, bf16[8,256,576]{2,1,0:T(8,128)(2,1)} %get-tuple-element.112.grad_ref, bf16[4,768,576]{2,1,0:T(8,128)(2,1)} %get-tuple-element.113.group_ref, bf16[768,1152]{1,0:T(8,128)(2,1)} %add_convert_fusion.refs_6_.rest_0_, ...), custom_call_target="tpu_custom_call" | custom-call | flops 1811939328 | bytes 8000000 | tf_op jit(solution)/shard_map/input_grad/pallas_call | solution.py:980
  429.7 7.3 %collective-permute-done.38 = bf16[96,1152]{1,0:T(8,128)(2,1)} collective-permute-done((bf16[96,1152]{1,0:T(8,128)(2,1)S(1)}, bf16[96,1152]{1,0:T(8,128)(2,1)}, u32[]{:S(2)}, u32[]{:S(2)}) %collective-permute-start.38) | collective-permute-done | bytes 221216 | tf_op jit(solution)/shard_map/ppermute | solution.py:1028
  471.7 12.6 %collective-permute-done.45.refs_0_ = f32[3,128,256]{2,1,0:T(8,128)} collective-permute-done((f32[3,128,256]{2,1,0:T(8,128)S(1)}, f32[3,128,256]{2,1,0:T(8,128)}, u32[]{:S(2)}, u32[]{:S(2)}) %collective-permute-start.45) | collective-permute-done | bytes 393248 | tf_op jit(solution)/shard_map/ppermute | solution.py:1028
  485.5 7.3 %all-gather.5.cloned.1.call-done.mine_ref = bf16[768,1152]{1,0:T(8,128)(2,1)} async-done(((bf16[192,1152]{1,0:T(8,128)(2,1)}), bf16[768,1152]{1,0:T(8,128)(2,1)}) %all-gather.5.cloned.1.call-update) | async-done | bytes 1769488 | tf_op jit(solution)/shard_map/all_gather | solution.py:1052
  501.7 34.6 %newton_schulz.1 = bf16[768,768]{1,0:T(8,128)(2,1)} custom-call(s32[1]{0:T(128)} %bitcast.49.which_ref, f32[2,6,128,256]{3,2,1,0:T(8,128)} %pad_maximum_fusion.1.packed_ref, bf16[768,1152]{1,0:T(8,128)(2,1)} %all-gather.5.cloned.1.call-done.mine_ref, bf16[768,1152]{1,0:T(8,128)(2,1)} %collective-permute-done.48.theirs_ref, ...), custom_call_target="tpu_custom_call" | custom-call | flops 36238786560 | bytes 7000000 | tf_op jit(solution)/shard_map/newton_schulz/pallas_call | solution.py:536
  544.1 10.8 %collective-permute-done.49.refs_1_ = bf16[384,768]{1,0:T(8,128)(2,1)} collective-permute-done((bf16[384,768]{1,0:T(8,128)(2,1)}, bf16[384,768]{1,0:T(8,128)(2,1)}, u32[]{:S(2)}, u32[]{:S(2)}) %collective-permute-start.49) | collective-permute-done | bytes 589856 | tf_op jit(solution)/shard_map/ppermute | solution.py:1028
  554.8 15.2 %collective-permute-done.50.refs_2_ = bf16[384,768]{1,0:T(8,128)(2,1)} collective-permute-done((bf16[384,768]{1,0:T(8,128)(2,1)}, bf16[384,768]{1,0:T(8,128)(2,1)}, u32[]{:S(2)}, u32[]{:S(2)}) %collective-permute-start.50) | collective-permute-done | bytes 589856 | tf_op jit(solution)/shard_map/ppermute | solution.py:1028
  574.8 14.0 %update.1 = (f32[768,1536]{1,0:T(8,128)}, f32[768,768]{1,0:T(8,128)}, f32[192,768]{1,0:T(8,128)}, f32[576,768]{1,0:T(8,128)}) custom-call(s32[2]{0:T(128)} %pad_add_fusion.3.place_ref, bf16[384,768]{1,0:T(8,128)(2,1)} %dynamic-slice_bitcast_fusion.refs_0_, bf16[384,768]{1,0:T(8,128)(2,1)} %collective-permute-done.49.refs_1_, ...), custom_call_target="tpu_custom_call" | custom-call | flops 3623878656 | bytes 28000000 | tf_op jit(solution)/shard_map/update/pallas_call | solution.py:623
  (303 shorter events, 229.2 us)
Async XLA Ops:
  46.2 42.3 %collective-permute-start.9 = (bf16[192,2304]{1,0:T(8,128)(2,1)}, bf16[192,2304]{1,0:T(8,128)(2,1)}, u32[]{:S(2)}, u32[]{:S(2)}) collective-permute-start(bf16[192,2304]{1,0:T(8,128)(2,1)} %pad_maximum_fusion.4.refs_1_), channel_id=1, source_target_pairs={{0,16},{1,17},{2,18},{3,19},{4,20},{5,21},{6,22},{7,23},{8,24},{9,... | collective-permute-start | bytes 2654216 | tf_op jit(solution)/shard_map/ppermute | solution.py:1028
  72.3 42.5 %all-to-all-start = ((bf16[8,128,1152]{2,1,0:T(8,128)(2,1)}), bf16[8,128,1152]{2,1,0:T(8,128)(2,1)}, u32[]{:S(2)}, u32[]{:S(2)}) async-start(bf16[8,128,1152]{2,1,0:T(8,128)(2,1)} %get-tuple-element.71), calls=%async_computation | async-start | bytes 4718592 | tf_op jit(solution)/shard_map/all_to_all | solution.py:1097
  76.7 73.2 %all-gather.3.cloned.1.call-start = ((), (), s32[]{:S(2)}) async-start(), calls=%async_computation.7 | async-start | bytes 4423680 | tf_op jit(solution)/shard_map/all_gather | solution.py:1109
  93.8 61.7 %collective-permute-start.10 = (bf16[768,2304]{1,0:T(8,128)(2,1)}, bf16[768,2304]{1,0:T(8,128)(2,1)}, u32[]{:S(2)}, u32[]{:S(2)}) collective-permute-start(bf16[768,2304]{1,0:T(8,128)(2,1)} %pad_maximum_fusion.own_ref), channel_id=1, source_target_pairs={{0,8},{1,9},{2,10},{3,11},{4,12},{5,13},{6,14},{7,15},{8,0},{9,1},... | collective-permute-start | bytes 10616840 | tf_op jit(solution)/shard_map/ppermute | solution.py:1028
  232.9 33.3 %collective-permute-start.15 = (bf16[2,2,1,2,96,896]{5,4,3,2,1,0:T(8,128)(2,1)}, bf16[2,2,1,2,96,896]{5,4,3,2,1,0:T(8,128)(2,1)S(1)}, u32[]{:S(2)}, u32[]{:S(2)}) collective-permute-start(bf16[2,2,1,2,96,896]{5,4,3,2,1,0:T(8,128)(2,1)} %bitcast.130), channel_id=1, source_target_pairs={{0,2},{1,3},{2,0},{3,1},{4,6},{5,7},{6,4},{7,5},{8,10},{9,11},{10,... | collective-permute-start | bytes 4128776 | tf_op jit(solution)/shard_map/ppermute | solution.py:1028
  233.0 35.3 %collective-permute-start.16 = (bf16[2,1,2,2,96,896]{5,4,3,2,1,0:T(8,128)(2,1)}, bf16[2,1,2,2,96,896]{5,4,3,2,1,0:T(8,128)(2,1)}, u32[]{:S(2)}, u32[]{:S(2)}) collective-permute-start(bf16[2,1,2,2,96,896]{5,4,3,2,1,0:T(8,128)(2,1)} %bitcast.128), channel_id=1, source_target_pairs={{0,4},{1,5},{2,6},{3,7},{4,0},{5,1},{6,2},{7,3},{8,12},{9,13},{10,... | collective-permute-start | bytes 4128776 | tf_op jit(solution)/shard_map/ppermute | solution.py:1028
  234.4 28.2 %collective-permute-start.17 = (bf16[2,2,2,1,96,768]{5,4,3,2,1,0:T(8,128)(2,1)}, bf16[2,2,2,1,96,768]{5,4,3,2,1,0:T(8,128)(2,1)}, u32[]{:S(2)}, u32[]{:S(2)}) collective-permute-start(bf16[2,2,2,1,96,768]{5,4,3,2,1,0:T(8,128)(2,1)} %bitcast.132), channel_id=1, source_target_pairs={{0,1},{1,0},{2,3},{3,2},{4,5},{5,4},{6,7},{7,6},{8,9},{9,8},{10,11... | collective-permute-start | bytes 3538952 | tf_op jit(solution)/shard_map/ppermute | solution.py:1028
  235.3 27.2 %collective-permute-start.18 = (f32[2,2880]{1,0:T(2,128)}, f32[2,2880]{1,0:T(2,128)S(1)}, u32[]{:S(2)}, u32[]{:S(2)}) collective-permute-start(f32[2,2880]{1,0:T(2,128)} %get-tuple-element.87.rest_3_.refs_6_), channel_id=1, source_target_pairs={{0,1},{1,0},{2,3},{3,2},{4,5},{5,4},{6,7},{7,6},{8,9},{9,8},{10,11... | collective-permute-start | bytes 69128 | tf_op jit(solution)/shard_map/ppermute | solution.py:1028
  257.6 55.4 %all-to-all-start.3 = ((bf16[8,128,384]{2,1,0:T(8,128)(2,1)}), bf16[8,128,384]{2,1,0:T(8,128)(2,1)}, u32[]{:S(2)}, u32[]{:S(2)}) async-start(bf16[8,128,384]{2,1,0:T(8,128)(2,1)} %attention_backward.3.refs_8_), calls=%async_computation.3 | async-start | bytes 1572864 | tf_op jit(solution)/shard_map/all_to_all | solution.py:1097
  273.2 30.1 %collective-permute-start.19 = (bf16[2,1,1,2,96,896]{5,4,3,2,1,0:T(8,128)(2,1)}, bf16[2,1,1,2,96,896]{5,4,3,2,1,0:T(8,128)(2,1)S(1)}, u32[]{:S(2)}, u32[]{:S(2)}) collective-permute-start(bf16[2,1,1,2,96,896]{5,4,3,2,1,0:T(8,128)(2,1)} %bitcast.140), channel_id=1, source_target_pairs={{0,4},{1,5},{2,6},{3,7},{4,0},{5,1},{6,2},{7,3},{8,12},{9,13},{10,... | collective-permute-start | bytes 2064392 | tf_op jit(solution)/shard_map/ppermute | solution.py:1028
  273.9 29.4 %collective-permute-start.20 = (bf16[2,1,2,1,96,896]{5,4,3,2,1,0:T(8,128)(2,1)}, bf16[2,1,2,1,96,896]{5,4,3,2,1,0:T(8,128)(2,1)S(1)}, u32[]{:S(2)}, u32[]{:S(2)}) collective-permute-start(bf16[2,1,2,1,96,896]{5,4,3,2,1,0:T(8,128)(2,1)} %bitcast.138), channel_id=1, source_target_pairs={{0,1},{1,0},{2,3},{3,2},{4,5},{5,4},{6,7},{7,6},{8,9},{9,8},{10,11... | collective-permute-start | bytes 2064392 | tf_op jit(solution)/shard_map/ppermute | solution.py:1028
  276.5 26.8 %collective-permute-start.21 = (bf16[2,2,1,1,96,768]{5,4,3,2,1,0:T(8,128)(2,1)}, bf16[2,2,1,1,96,768]{5,4,3,2,1,0:T(8,128)(2,1)S(1)}, u32[]{:S(2)}, u32[]{:S(2)}) collective-permute-start(bf16[2,2,1,1,96,768]{5,4,3,2,1,0:T(8,128)(2,1)} %bitcast.143), channel_id=1, source_target_pairs={{0,2},{1,3},{2,0},{3,1},{4,6},{5,7},{6,4},{7,5},{8,10},{9,11},{10,... | collective-permute-start | bytes 1769480 | tf_op jit(solution)/shard_map/ppermute | solution.py:1028
  307.7 30.1 %collective-permute-start.23 = (bf16[2,1,1,1,96,896]{5,4,3,2,1,0:T(8,128)(2,1)}, bf16[2,1,1,1,96,896]{5,4,3,2,1,0:T(8,128)(2,1)S(1)}, u32[]{:S(2)}, u32[]{:S(2)}) collective-permute-start(bf16[2,1,1,1,96,896]{5,4,3,2,1,0:T(8,128)(2,1)} %bitcast.147), channel_id=1, source_target_pairs={{0,1},{1,0},{2,3},{3,2},{4,5},{5,4},{6,7},{7,6},{8,9},{9,8},{10,11... | collective-permute-start | bytes 1032200 | tf_op jit(solution)/shard_map/ppermute | solution.py:1028
  309.0 28.8 %collective-permute-start.24 = (bf16[2,1,1,1,96,896]{5,4,3,2,1,0:T(8,128)(2,1)}, bf16[2,1,1,1,96,896]{5,4,3,2,1,0:T(8,128)(2,1)S(1)}, u32[]{:S(2)}, u32[]{:S(2)}) collective-permute-start(bf16[2,1,1,1,96,896]{5,4,3,2,1,0:T(8,128)(2,1)} %bitcast.145), channel_id=1, source_target_pairs={{0,2},{1,3},{2,0},{3,1},{4,6},{5,7},{6,4},{7,5},{8,10},{9,11},{10,... | collective-permute-start | bytes 1032200 | tf_op jit(solution)/shard_map/ppermute | solution.py:1028
  311.0 26.8 %collective-permute-start.25 = (bf16[2,1,1,1,96,768]{5,4,3,2,1,0:T(8,128)(2,1)}, bf16[2,1,1,1,96,768]{5,4,3,2,1,0:T(8,128)(2,1)}, u32[]{:S(2)}, u32[]{:S(2)}) collective-permute-start(bf16[2,1,1,1,96,768]{5,4,3,2,1,0:T(8,128)(2,1)} %bitcast.149), channel_id=1, source_target_pairs={{0,4},{1,5},{2,6},{3,7},{4,0},{5,1},{6,2},{7,3},{8,12},{9,13},{10,... | collective-permute-start | bytes 884744 | tf_op jit(solution)/shard_map/ppermute | solution.py:1028
  312.4 25.3 %collective-permute-start.26 = (f32[2,2880]{1,0:T(2,128)}, f32[2,2880]{1,0:T(2,128)S(1)}, u32[]{:S(2)}, u32[]{:S(2)}) collective-permute-start(f32[2,2880]{1,0:T(2,128)} %get-tuple-element.101.rest_3_.refs_6_), channel_id=1, source_target_pairs={{0,4},{1,5},{2,6},{3,7},{4,0},{5,1},{6,2},{7,3},{8,12},{9,13},{10,... | collective-permute-start | bytes 69128 | tf_op jit(solution)/shard_map/ppermute | solution.py:1028
  313.0 28.2 %all-to-all-start.4 = ((bf16[8,128,384]{2,1,0:T(8,128)(2,1)}), bf16[8,128,384]{2,1,0:T(8,128)(2,1)S(1)}, u32[]{:S(2)}, u32[]{:S(2)}) async-start(bf16[8,128,384]{2,1,0:T(8,128)(2,1)} %attention_backward.4.refs_8_), calls=%async_computation.4 | async-start | bytes 1572864 | tf_op jit(solution)/shard_map/all_to_all | solution.py:1097
  341.2 27.9 %all-to-all-start.5 = ((bf16[8,128,384]{2,1,0:T(8,128)(2,1)}), bf16[8,128,384]{2,1,0:T(8,128)(2,1)}, u32[]{:S(2)}, u32[]{:S(2)}) async-start(bf16[8,128,384]{2,1,0:T(8,128)(2,1)} %after.10), calls=%async_computation.5 | async-start | bytes 1572864 | tf_op jit(solution)/shard_map/all_to_all | solution.py:1097
  346.4 79.7 %reduce-scatter.2.cloned.1.call-start = ((), (), s32[]{:S(2)}) async-start(), calls=%async_computation.8 | async-start | bytes 2211840 | tf_op jit(solution)/shard_map/reduce_scatter | solution.py:1214
  385.7 107.1 %all-gather.5.cloned.1.call-start = ((), (), s32[]{:S(2)}) async-start(), calls=%async_computation.9 | async-start | bytes 2211840 | tf_op jit(solution)/shard_map/all_gather | solution.py:1052
  415.3 25.5 %collective-permute-start.40 = (bf16[2,2,1,96,896]{4,3,2,1,0:T(8,128)(2,1)}, bf16[2,2,1,96,896]{4,3,2,1,0:T(8,128)(2,1)S(1)}, u32[]{:S(2)}, u32[]{:S(2)}) collective-permute-start(bf16[2,2,1,96,896]{4,3,2,1,0:T(8,128)(2,1)} %get-tuple-element.119.rest_1_.refs_0_), channel_id=1, source_target_pairs={{0,1},{1,0},{2,3},{3,2},{4,5},{5,4},{6,7},{7,6},{8,9},{9,8},{10,11... | collective-permute-start | bytes 2064392 | tf_op jit(solution)/shard_map/ppermute | solution.py:1028
  539.6 30.4 %collective-permute-start.50 = (bf16[384,768]{1,0:T(8,128)(2,1)}, bf16[384,768]{1,0:T(8,128)(2,1)}, u32[]{:S(2)}, u32[]{:S(2)}) collective-permute-start(bf16[384,768]{1,0:T(8,128)(2,1)} %dynamic-slice_bitcast_fusion.refs_0_), channel_id=1, source_target_pairs={{0,4},{1,5},{2,6},{3,7},{4,0},{5,1},{6,2},{7,3},{8,12},{9,13},{10,... | collective-permute-start | bytes 1769480 | tf_op jit(solution)/shard_map/ppermute | solution.py:1028
  543.7 26.3 %collective-permute-start.51 = (bf16[384,768]{1,0:T(8,128)(2,1)}, bf16[384,768]{1,0:T(8,128)(2,1)}, u32[]{:S(2)}, u32[]{:S(2)}) collective-permute-start(bf16[384,768]{1,0:T(8,128)(2,1)} %dynamic-slice_bitcast_fusion.refs_0_), channel_id=1, source_target_pairs={{0,6},{1,7},{2,4},{3,5},{4,2},{5,3},{6,0},{7,1},{8,14},{9,15},{10,... | collective-permute-start | bytes 1769480 | tf_op jit(solution)/shard_map/ppermute | solution.py:1028
  544.0 30.8 %collective-permute-start.52 = (bf16[384,768]{1,0:T(8,128)(2,1)}, bf16[384,768]{1,0:T(8,128)(2,1)}, u32[]{:S(2)}, u32[]{:S(2)}) collective-permute-start(bf16[384,768]{1,0:T(8,128)(2,1)} %dynamic-slice_bitcast_fusion.refs_0_), channel_id=1, source_target_pairs={{0,8},{1,9},{2,10},{3,11},{4,12},{5,13},{6,14},{7,15},{8,0},{9,1},... | collective-permute-start | bytes 1769480 | tf_op jit(solution)/shard_map/ppermute | solution.py:1028
  (88 other events, 1155.9 us)
Sparse Core Ops, SparseCore 0:
  88.7 57.0 all-gather.2
  385.8 40.2 reduce-scatter.1
  459.6 33.1 all-gather.4

commit v2 on v1

--- a/solution.py
+++ b/solution.py
@@ -742,7 +742,7 @@
     grads_a = (keep_a, send_a)
     grads_b = (keep_b, send_b)
     down_at = 2 * width
-    part = rows // 2
+    part = rows
 
     def vec(i):
         return vec_ref[i : i + 1, :]

time: 602 us -> 600 us (level)
  no operation moved by 1% of the time
where the time goes in v2:
time: 600 us; the launch traced here: 593 us
  Pallas kernels  247 us (41%)
  waiting for transfers between devices  165 us (28%)
  starting transfers between devices  90.7 us (15%)
  other arithmetic  42.4 us (7%)
  local copies, waits for them, and re-layouts  34.5 us (6%)
  between operations  14.8 us (2%)
    ppermute x56, waiting for transfers between devices, swap(): return lax.ppermute(value, AXES, pairs)  125 us
    pallas_call x3, Pallas kernels, attention_backward(): pl.pallas_call(functools.partial(attention_backward_kernel, rows, q_block...  64.6 us
    ppermute x56, starting transfers between devices, swap(): return lax.ppermute(value, AXES, pairs)  62.7 us
    pallas_call x1, Pallas kernels, feed_forward(): pl.pallas_call(functools.partial(feed_forward_kernel, groups), out_shape=...  40.4 us
    pallas_call x1, Pallas kernels, attention_forward(): pl.pallas_call(functools.partial(attention_forward_kernel, rows, q_blocks...  35.1 us
    pallas_call x1, Pallas kernels, newton_schulz(): pl.pallas_call(functools.partial(newton_schulz_kernel, whole), out_shape=...  34.6 us
    all_to_all x6, waiting for transfers between devices, exchange(): return lax.all_to_all(blocks, ('seq', 'head'), 0, 0, tiled=True)  31.6 us
    all_to_all x6, starting transfers between devices, exchange(): return lax.all_to_all(blocks, ('seq', 'head'), 0, 0, tiled=True)  27.1 us
  transfers between devices with their start and end apart: 65, of which 29 were waited for; matrix products, arithmetic and copies ran while one was open for 9% of the time, Pallas kernels for 25%

profile of v2, /device:TPU:0, one launch (start us, length us, event | category | flops | bytes accessed | tf_op | source)
XLA Modules:
  0.0 593.5 jit_solution(484582865976530653)
XLA Ops:
  31.1 5.8 collective-permute-done.5
  64.6 7.8 %project.1 = (bf16[8,128,1152]{2,1,0:T(8,128)(2,1)}, bf16[4,768,576]{2,1,0:T(8,128)(2,1)}, bf16[768,768]{1,0:T(8,128)(2,1)}) custom-call(s32[5]{0:T(128)} %pad_add_fusion.info_ref, f32[16,768]{1,0:T(8,128)} %pad_convert_fusion.vec_ref, bf16[512,768]{1,0:T(8,128)(2,1)} %bitcast.135, bf16[768,768]{1,0:T(8,128)(2,1)} %pad_maximum_fusion.2.own_ref, ...), custom_call_target="tpu_custom_call" | custom-call | flops 1811939328 | bytes 16000000 | tf_op jit(solution)/shard_map/project/pallas_call | solution.py:668
  77.3 11.3 %collective-permute-done.9.refs_0_ = bf16[192,2304]{1,0:T(8,128)(2,1)} collective-permute-done((bf16[192,2304]{1,0:T(8,128)(2,1)}, bf16[192,2304]{1,0:T(8,128)(2,1)}, u32[]{:S(2)}, u32[]{:S(2)}) %collective-permute-start.9) | collective-permute-done | bytes 884768 | tf_op jit(solution)/shard_map/ppermute | solution.py:1028
  96.3 18.5 %all-to-all-done.qkv_ref = bf16[8,128,1152]{2,1,0:T(8,128)(2,1)} async-done(((bf16[8,128,1152]{2,1,0:T(8,128)(2,1)}), bf16[8,128,1152]{2,1,0:T(8,128)(2,1)}, u32[]{:S(2)}, u32[]{:S(2)}) %all-to-all-start) | async-done | bytes 2359328 | tf_op jit(solution)/shard_map/all_to_all | solution.py:1097
  114.8 35.1 %attention_forward.1 = (f32[2048,192]{1,0:T(8,128)}, bf16[8,128,384]{2,1,0:T(8,128)(2,1)}, f32[2048,128]{1,0:T(8,128)}) custom-call(s32[2]{0:T(128)} %pad_add_fusion.1.info_ref, f32[3]{0:T(128)} %exponential_multiply_fusion.slope_ref, bf16[8,128,1152]{2,1,0:T(8,128)(2,1)} %all-to-all-done.qkv_ref), custom_call_target="tpu_custom_call" | custom-call | flops 12884901888 | bytes 6000000 | tf_op jit(solution)/shard_map/attention_forward/pallas_call | solution.py:298
  149.9 5.4 all-to-all-start.1
  155.4 13.1 %all-to-all-done.1.ctx_ref = bf16[8,128,384]{2,1,0:T(8,128)(2,1)S(1)} async-done(((bf16[8,128,384]{2,1,0:T(8,128)(2,1)}), bf16[8,128,384]{2,1,0:T(8,128)(2,1)S(1)}, u32[]{:S(2)}, u32[]{:S(2)}) %all-to-all-start.1) | async-done | bytes 786464 | tf_op jit(solution)/shard_map/all_to_all | solution.py:1097
  169.3 40.4 %feed_forward.1 = (bf16[512,768]{1,0:T(8,128)(2,1)}, f32[512,768]{1,0:T(8,128)}, bf16[8,128,384]{2,1,0:T(8,128)(2,1)}, f32[16,768]{1,0:T(8,128)}, bf16[2,768,179...) custom-call(s32[5]{0:T(128)} %pad_add_fusion.info_ref, ...), custom_call_target="tpu_custom_call" | custom-call | flops 18119393280 | bytes 34000000 | tf_op jit(solution)/shard_map/feed_forward/pallas_call | solution.py:876
  222.6 8.4 %sum_split.4 = (bf16[2,2,2,96,896]{4,3,2,1,0:T(8,128)(2,1)}, bf16[2,2,2,96,896]{4,3,2,1,0:T(8,128)(2,1)}, bf16[2,2,2,96,896]{4,3,2,1,0:T(8,128)(2,1)}, bf16[2,2,...) custom-call(s32[3]{0:T(128)} %pad_add_fusion.2.bits_ref, ...), custom_call_target="tpu_custom_call" | custom-call | bytes 23592960 | tf_op jit(solution)/shard_map/sum_split/pallas_call | solution.py:119
  234.5 21.2 %attention_backward.3.refs_8_ = bf16[8,128,384]{2,1,0:T(8,128)(2,1)} custom-call(s32[2]{0:T(128)} %pad_add_fusion.1.info_ref, f32[3]{0:T(128)} %exponential_multiply_fusion.slope_ref, bf16[8,128,1152]{2,1,0:T(8,128)(2,1)} %all-to-all-done.qkv_ref, f32[2048,192]{1,0:T(8,128)} %get-tuple-element.76.att_ref, f32[2048,128]{1,0:T(8,128)} %get-tuple-element.77.log_ref, ...), custom_call_target="tpu_custom_call" | custom-call | flops 21474836480 | bytes 7000000 | tf_op jit(solution)/shard_map/attention_backward/pallas_call | solution.py:414
  279.1 22.2 %attention_backward.4.refs_8_ = bf16[8,128,384]{2,1,0:T(8,128)(2,1)} custom-call(s32[2]{0:T(128)} %pad_add_fusion.1.info_ref, f32[3]{0:T(128)} %exponential_multiply_fusion.slope_ref, bf16[8,128,1152]{2,1,0:T(8,128)(2,1)} %all-to-all-done.qkv_ref, f32[2048,192]{1,0:T(8,128)} %get-tuple-element.76.att_ref, f32[2048,128]{1,0:T(8,128)} %get-tuple-element.77.log_ref, ...), custom_call_target="tpu_custom_call" | custom-call | flops 21474836480 | bytes 7000000 | tf_op jit(solution)/shard_map/attention_backward/pallas_call | solution.py:414
  314.7 21.2 %attention_backward.5.refs_8_.refs_0_ = bf16[8,128,384]{2,1,0:T(8,128)(2,1)} custom-call(s32[2]{0:T(128)} %pad_add_fusion.1.info_ref, f32[3]{0:T(128)} %exponential_multiply_fusion.slope_ref, bf16[8,128,1152]{2,1,0:T(8,128)(2,1)} %all-to-all-done.qkv_ref, f32[2048,192]{1,0:T(8,128)} %get-tuple-element.76.att_ref, f32[2048,128]{1,0:T(8,128)} %get-tuple-element.77.log_ref, ...), custom_call_target="tpu_custom_call" | custom-call | flops 21474836480 | bytes 7000000 | tf_op jit(solution)/shard_map/attention_backward/pallas_call | solution.py:414
  353.8 7.0 %collective-permute-done.29 = bf16[96,768]{1,0:T(8,128)(2,1)S(1)} collective-permute-done((bf16[96,768]{1,0:T(8,128)(2,1)}, bf16[96,768]{1,0:T(8,128)(2,1)S(1)}, u32[]{:S(2)}, u32[]{:S(2)}) %collective-permute-start.29) | collective-permute-done | bytes 147488 | tf_op jit(solution)/shard_map/ppermute | solution.py:1028
  367.0 9.5 %qkv_grad.1 = (bf16[8,256,576]{2,1,0:T(8,128)(2,1)}, bf16[768,1152]{1,0:T(8,128)(2,1)}, bf16[768,1152]{1,0:T(8,128)(2,1)}) custom-call(s32[5]{0:T(128)} %pad_add_fusion.info_ref, bf16[512,768]{1,0:T(8,128)(2,1)} %bitcast.137, bf16[8,128,384]{2,1,0:T(8,128)(2,1)} %all-to-all-done.3.rest_4_.refs_0_, bf16[8,128,384]{2,1,0:T(8,128)(2,1)} %copy-done.18, ...), custom_call_target="tpu_custom_call" | custom-call | flops 1811939328 | bytes 9000000 | tf_op jit(solution)/shard_map/qkv_grad/pallas_call | solution.py:949
  399.7 8.4 %collective-permute-done.37.refs_5_ = bf16[1,1,2,96,768]{4,3,2,1,0:T(8,128)(2,1)S(1)} collective-permute-done((bf16[1,1,2,96,768]{4,3,2,1,0:T(8,128)(2,1)}, bf16[1,1,2,96,768]{4,3,2,1,0:T(8,128)(2,1)S(1)}, u32[]{:S(2)}, u32[]{:S(2)}) %collective-permute-start.37) | collective-permute-done | bytes 294944 | tf_op jit(solution)/shard_map/ppermute | solution.py:1028
  416.7 6.9 %input_grad.1.refs_1_.refs_6_ = bf16[512,768]{1,0:T(8,128)(2,1)} custom-call(f32[512,768]{1,0:T(8,128)} %get-tuple-element.75.one_ref, bf16[8,256,576]{2,1,0:T(8,128)(2,1)} %get-tuple-element.112.grad_ref, bf16[4,768,576]{2,1,0:T(8,128)(2,1)} %get-tuple-element.113.group_ref, bf16[768,1152]{1,0:T(8,128)(2,1)} %add_convert_fusion.refs_6_.rest_0_, ...), custom_call_target="tpu_custom_call" | custom-call | flops 1811939328 | bytes 8000000 | tf_op jit(solution)/shard_map/input_grad/pallas_call | solution.py:980
  427.6 7.3 %collective-permute-done.38 = bf16[96,1152]{1,0:T(8,128)(2,1)} collective-permute-done((bf16[96,1152]{1,0:T(8,128)(2,1)S(1)}, bf16[96,1152]{1,0:T(8,128)(2,1)}, u32[]{:S(2)}, u32[]{:S(2)}) %collective-permute-start.38) | collective-permute-done | bytes 221216 | tf_op jit(solution)/shard_map/ppermute | solution.py:1028
  443.8 5.3 upper_gram.1.refs_1_
  469.6 12.9 %collective-permute-done.45.refs_0_ = f32[3,128,256]{2,1,0:T(8,128)} collective-permute-done((f32[3,128,256]{2,1,0:T(8,128)S(1)}, f32[3,128,256]{2,1,0:T(8,128)}, u32[]{:S(2)}, u32[]{:S(2)}) %collective-permute-start.45) | collective-permute-done | bytes 393248 | tf_op jit(solution)/shard_map/ppermute | solution.py:1028
  483.6 7.1 %all-gather.5.cloned.1.call-done.mine_ref = bf16[768,1152]{1,0:T(8,128)(2,1)} async-done(((bf16[192,1152]{1,0:T(8,128)(2,1)}), bf16[768,1152]{1,0:T(8,128)(2,1)}) %all-gather.5.cloned.1.call-update) | async-done | bytes 1769488 | tf_op jit(solution)/shard_map/all_gather | solution.py:1052
  499.9 34.6 %newton_schulz.1 = bf16[768,768]{1,0:T(8,128)(2,1)} custom-call(s32[1]{0:T(128)} %bitcast.49.which_ref, f32[2,6,128,256]{3,2,1,0:T(8,128)} %pad_maximum_fusion.1.packed_ref, bf16[768,1152]{1,0:T(8,128)(2,1)} %all-gather.5.cloned.1.call-done.mine_ref, bf16[768,1152]{1,0:T(8,128)(2,1)} %collective-permute-done.48.theirs_ref, ...), custom_call_target="tpu_custom_call" | custom-call | flops 36238786560 | bytes 7000000 | tf_op jit(solution)/shard_map/newton_schulz/pallas_call | solution.py:536
  541.9 11.1 %collective-permute-done.49.refs_1_ = bf16[384,768]{1,0:T(8,128)(2,1)} collective-permute-done((bf16[384,768]{1,0:T(8,128)(2,1)}, bf16[384,768]{1,0:T(8,128)(2,1)}, u32[]{:S(2)}, u32[]{:S(2)}) %collective-permute-start.49) | collective-permute-done | bytes 589856 | tf_op jit(solution)/shard_map/ppermute | solution.py:1028
  553.0 14.9 %collective-permute-done.50.refs_2_ = bf16[384,768]{1,0:T(8,128)(2,1)} collective-permute-done((bf16[384,768]{1,0:T(8,128)(2,1)}, bf16[384,768]{1,0:T(8,128)(2,1)}, u32[]{:S(2)}, u32[]{:S(2)}) %collective-permute-start.50) | collective-permute-done | bytes 589856 | tf_op jit(solution)/shard_map/ppermute | solution.py:1028
  572.7 14.0 %update.1 = (f32[768,1536]{1,0:T(8,128)}, f32[768,768]{1,0:T(8,128)}, f32[192,768]{1,0:T(8,128)}, f32[576,768]{1,0:T(8,128)}) custom-call(s32[2]{0:T(128)} %pad_add_fusion.3.place_ref, bf16[384,768]{1,0:T(8,128)(2,1)} %dynamic-slice_bitcast_fusion.refs_0_, bf16[384,768]{1,0:T(8,128)(2,1)} %collective-permute-done.49.refs_1_, ...), custom_call_target="tpu_custom_call" | custom-call | flops 3623878656 | bytes 28000000 | tf_op jit(solution)/shard_map/update/pallas_call | solution.py:623
  (303 shorter events, 229.2 us)
Async XLA Ops:
  46.2 42.3 %collective-permute-start.9 = (bf16[192,2304]{1,0:T(8,128)(2,1)}, bf16[192,2304]{1,0:T(8,128)(2,1)}, u32[]{:S(2)}, u32[]{:S(2)}) collective-permute-start(bf16[192,2304]{1,0:T(8,128)(2,1)} %pad_maximum_fusion.4.refs_1_), channel_id=1, source_target_pairs={{0,16},{1,17},{2,18},{3,19},{4,20},{5,21},{6,22},{7,23},{8,24},{9,... | collective-permute-start | bytes 2654216 | tf_op jit(solution)/shard_map/ppermute | solution.py:1028
  72.3 42.5 %all-to-all-start = ((bf16[8,128,1152]{2,1,0:T(8,128)(2,1)}), bf16[8,128,1152]{2,1,0:T(8,128)(2,1)}, u32[]{:S(2)}, u32[]{:S(2)}) async-start(bf16[8,128,1152]{2,1,0:T(8,128)(2,1)} %get-tuple-element.71), calls=%async_computation | async-start | bytes 4718592 | tf_op jit(solution)/shard_map/all_to_all | solution.py:1097
  76.7 73.2 %all-gather.3.cloned.1.call-start = ((), (), s32[]{:S(2)}) async-start(), calls=%async_computation.7 | async-start | bytes 4423680 | tf_op jit(solution)/shard_map/all_gather | solution.py:1109
  93.8 61.6 %collective-permute-start.10 = (bf16[768,2304]{1,0:T(8,128)(2,1)}, bf16[768,2304]{1,0:T(8,128)(2,1)}, u32[]{:S(2)}, u32[]{:S(2)}) collective-permute-start(bf16[768,2304]{1,0:T(8,128)(2,1)} %pad_maximum_fusion.own_ref), channel_id=1, source_target_pairs={{0,8},{1,9},{2,10},{3,11},{4,12},{5,13},{6,14},{7,15},{8,0},{9,1},... | collective-permute-start | bytes 10616840 | tf_op jit(solution)/shard_map/ppermute | solution.py:1028
  231.0 33.3 %collective-permute-start.15 = (bf16[2,2,1,2,96,896]{5,4,3,2,1,0:T(8,128)(2,1)}, bf16[2,2,1,2,96,896]{5,4,3,2,1,0:T(8,128)(2,1)S(1)}, u32[]{:S(2)}, u32[]{:S(2)}) collective-permute-start(bf16[2,2,1,2,96,896]{5,4,3,2,1,0:T(8,128)(2,1)} %bitcast.130), channel_id=1, source_target_pairs={{0,2},{1,3},{2,0},{3,1},{4,6},{5,7},{6,4},{7,5},{8,10},{9,11},{10,... | collective-permute-start | bytes 4128776 | tf_op jit(solution)/shard_map/ppermute | solution.py:1028
  231.1 35.3 %collective-permute-start.16 = (bf16[2,1,2,2,96,896]{5,4,3,2,1,0:T(8,128)(2,1)}, bf16[2,1,2,2,96,896]{5,4,3,2,1,0:T(8,128)(2,1)}, u32[]{:S(2)}, u32[]{:S(2)}) collective-permute-start(bf16[2,1,2,2,96,896]{5,4,3,2,1,0:T(8,128)(2,1)} %bitcast.128), channel_id=1, source_target_pairs={{0,4},{1,5},{2,6},{3,7},{4,0},{5,1},{6,2},{7,3},{8,12},{9,13},{10,... | collective-permute-start | bytes 4128776 | tf_op jit(solution)/shard_map/ppermute | solution.py:1028
  232.5 28.2 %collective-permute-start.17 = (bf16[2,2,2,1,96,768]{5,4,3,2,1,0:T(8,128)(2,1)}, bf16[2,2,2,1,96,768]{5,4,3,2,1,0:T(8,128)(2,1)}, u32[]{:S(2)}, u32[]{:S(2)}) collective-permute-start(bf16[2,2,2,1,96,768]{5,4,3,2,1,0:T(8,128)(2,1)} %bitcast.132), channel_id=1, source_target_pairs={{0,1},{1,0},{2,3},{3,2},{4,5},{5,4},{6,7},{7,6},{8,9},{9,8},{10,11... | collective-permute-start | bytes 3538952 | tf_op jit(solution)/shard_map/ppermute | solution.py:1028
  233.4 27.2 %collective-permute-start.18 = (f32[2,2880]{1,0:T(2,128)}, f32[2,2880]{1,0:T(2,128)S(1)}, u32[]{:S(2)}, u32[]{:S(2)}) collective-permute-start(f32[2,2880]{1,0:T(2,128)} %get-tuple-element.87.rest_3_.refs_6_), channel_id=1, source_target_pairs={{0,1},{1,0},{2,3},{3,2},{4,5},{5,4},{6,7},{7,6},{8,9},{9,8},{10,11... | collective-permute-start | bytes 69128 | tf_op jit(solution)/shard_map/ppermute | solution.py:1028
  255.7 55.4 %all-to-all-start.3 = ((bf16[8,128,384]{2,1,0:T(8,128)(2,1)}), bf16[8,128,384]{2,1,0:T(8,128)(2,1)}, u32[]{:S(2)}, u32[]{:S(2)}) async-start(bf16[8,128,384]{2,1,0:T(8,128)(2,1)} %attention_backward.3.refs_8_), calls=%async_computation.3 | async-start | bytes 1572864 | tf_op jit(solution)/shard_map/all_to_all | solution.py:1097
  271.3 30.1 %collective-permute-start.19 = (bf16[2,1,1,2,96,896]{5,4,3,2,1,0:T(8,128)(2,1)}, bf16[2,1,1,2,96,896]{5,4,3,2,1,0:T(8,128)(2,1)S(1)}, u32[]{:S(2)}, u32[]{:S(2)}) collective-permute-start(bf16[2,1,1,2,96,896]{5,4,3,2,1,0:T(8,128)(2,1)} %bitcast.140), channel_id=1, source_target_pairs={{0,4},{1,5},{2,6},{3,7},{4,0},{5,1},{6,2},{7,3},{8,12},{9,13},{10,... | collective-permute-start | bytes 2064392 | tf_op jit(solution)/shard_map/ppermute | solution.py:1028
  272.0 29.4 %collective-permute-start.20 = (bf16[2,1,2,1,96,896]{5,4,3,2,1,0:T(8,128)(2,1)}, bf16[2,1,2,1,96,896]{5,4,3,2,1,0:T(8,128)(2,1)S(1)}, u32[]{:S(2)}, u32[]{:S(2)}) collective-permute-start(bf16[2,1,2,1,96,896]{5,4,3,2,1,0:T(8,128)(2,1)} %bitcast.138), channel_id=1, source_target_pairs={{0,1},{1,0},{2,3},{3,2},{4,5},{5,4},{6,7},{7,6},{8,9},{9,8},{10,11... | collective-permute-start | bytes 2064392 | tf_op jit(solution)/shard_map/ppermute | solution.py:1028
  274.8 26.5 %collective-permute-start.21 = (bf16[2,2,1,1,96,768]{5,4,3,2,1,0:T(8,128)(2,1)}, bf16[2,2,1,1,96,768]{5,4,3,2,1,0:T(8,128)(2,1)S(1)}, u32[]{:S(2)}, u32[]{:S(2)}) collective-permute-start(bf16[2,2,1,1,96,768]{5,4,3,2,1,0:T(8,128)(2,1)} %bitcast.143), channel_id=1, source_target_pairs={{0,2},{1,3},{2,0},{3,1},{4,6},{5,7},{6,4},{7,5},{8,10},{9,11},{10,... | collective-permute-start | bytes 1769480 | tf_op jit(solution)/shard_map/ppermute | solution.py:1028
  305.8 30.1 %collective-permute-start.23 = (bf16[2,1,1,1,96,896]{5,4,3,2,1,0:T(8,128)(2,1)}, bf16[2,1,1,1,96,896]{5,4,3,2,1,0:T(8,128)(2,1)S(1)}, u32[]{:S(2)}, u32[]{:S(2)}) collective-permute-start(bf16[2,1,1,1,96,896]{5,4,3,2,1,0:T(8,128)(2,1)} %bitcast.147), channel_id=1, source_target_pairs={{0,1},{1,0},{2,3},{3,2},{4,5},{5,4},{6,7},{7,6},{8,9},{9,8},{10,11... | collective-permute-start | bytes 1032200 | tf_op jit(solution)/shard_map/ppermute | solution.py:1028
  307.1 28.8 %collective-permute-start.24 = (bf16[2,1,1,1,96,896]{5,4,3,2,1,0:T(8,128)(2,1)}, bf16[2,1,1,1,96,896]{5,4,3,2,1,0:T(8,128)(2,1)S(1)}, u32[]{:S(2)}, u32[]{:S(2)}) collective-permute-start(bf16[2,1,1,1,96,896]{5,4,3,2,1,0:T(8,128)(2,1)} %bitcast.145), channel_id=1, source_target_pairs={{0,2},{1,3},{2,0},{3,1},{4,6},{5,7},{6,4},{7,5},{8,10},{9,11},{10,... | collective-permute-start | bytes 1032200 | tf_op jit(solution)/shard_map/ppermute | solution.py:1028
  309.1 26.8 %collective-permute-start.25 = (bf16[2,1,1,1,96,768]{5,4,3,2,1,0:T(8,128)(2,1)}, bf16[2,1,1,1,96,768]{5,4,3,2,1,0:T(8,128)(2,1)}, u32[]{:S(2)}, u32[]{:S(2)}) collective-permute-start(bf16[2,1,1,1,96,768]{5,4,3,2,1,0:T(8,128)(2,1)} %bitcast.149), channel_id=1, source_target_pairs={{0,4},{1,5},{2,6},{3,7},{4,0},{5,1},{6,2},{7,3},{8,12},{9,13},{10,... | collective-permute-start | bytes 884744 | tf_op jit(solution)/shard_map/ppermute | solution.py:1028
  310.5 25.3 %collective-permute-start.26 = (f32[2,2880]{1,0:T(2,128)}, f32[2,2880]{1,0:T(2,128)S(1)}, u32[]{:S(2)}, u32[]{:S(2)}) collective-permute-start(f32[2,2880]{1,0:T(2,128)} %get-tuple-element.101.rest_3_.refs_6_), channel_id=1, source_target_pairs={{0,4},{1,5},{2,6},{3,7},{4,0},{5,1},{6,2},{7,3},{8,12},{9,13},{10,... | collective-permute-start | bytes 69128 | tf_op jit(solution)/shard_map/ppermute | solution.py:1028
  311.1 28.2 %all-to-all-start.4 = ((bf16[8,128,384]{2,1,0:T(8,128)(2,1)}), bf16[8,128,384]{2,1,0:T(8,128)(2,1)S(1)}, u32[]{:S(2)}, u32[]{:S(2)}) async-start(bf16[8,128,384]{2,1,0:T(8,128)(2,1)} %attention_backward.4.refs_8_), calls=%async_computation.4 | async-start | bytes 1572864 | tf_op jit(solution)/shard_map/all_to_all | solution.py:1097
  339.3 27.7 %all-to-all-start.5 = ((bf16[8,128,384]{2,1,0:T(8,128)(2,1)}), bf16[8,128,384]{2,1,0:T(8,128)(2,1)}, u32[]{:S(2)}, u32[]{:S(2)}) async-start(bf16[8,128,384]{2,1,0:T(8,128)(2,1)} %after.10), calls=%async_computation.5 | async-start | bytes 1572864 | tf_op jit(solution)/shard_map/all_to_all | solution.py:1097
  344.5 79.6 %reduce-scatter.2.cloned.1.call-start = ((), (), s32[]{:S(2)}) async-start(), calls=%async_computation.8 | async-start | bytes 2211840 | tf_op jit(solution)/shard_map/reduce_scatter | solution.py:1214
  383.6 107.1 %all-gather.5.cloned.1.call-start = ((), (), s32[]{:S(2)}) async-start(), calls=%async_computation.9 | async-start | bytes 2211840 | tf_op jit(solution)/shard_map/all_gather | solution.py:1052
  413.2 25.5 %collective-permute-start.40 = (bf16[2,2,1,96,896]{4,3,2,1,0:T(8,128)(2,1)}, bf16[2,2,1,96,896]{4,3,2,1,0:T(8,128)(2,1)S(1)}, u32[]{:S(2)}, u32[]{:S(2)}) collective-permute-start(bf16[2,2,1,96,896]{4,3,2,1,0:T(8,128)(2,1)} %get-tuple-element.119.rest_1_.refs_0_), channel_id=1, source_target_pairs={{0,1},{1,0},{2,3},{3,2},{4,5},{5,4},{6,7},{7,6},{8,9},{9,8},{10,11... | collective-permute-start | bytes 2064392 | tf_op jit(solution)/shard_map/ppermute | solution.py:1028
  537.3 30.7 %collective-permute-start.50 = (bf16[384,768]{1,0:T(8,128)(2,1)}, bf16[384,768]{1,0:T(8,128)(2,1)}, u32[]{:S(2)}, u32[]{:S(2)}) collective-permute-start(bf16[384,768]{1,0:T(8,128)(2,1)} %dynamic-slice_bitcast_fusion.refs_0_), channel_id=1, source_target_pairs={{0,4},{1,5},{2,6},{3,7},{4,0},{5,1},{6,2},{7,3},{8,12},{9,13},{10,... | collective-permute-start | bytes 1769480 | tf_op jit(solution)/shard_map/ppermute | solution.py:1028
  541.6 26.4 %collective-permute-start.51 = (bf16[384,768]{1,0:T(8,128)(2,1)}, bf16[384,768]{1,0:T(8,128)(2,1)}, u32[]{:S(2)}, u32[]{:S(2)}) collective-permute-start(bf16[384,768]{1,0:T(8,128)(2,1)} %dynamic-slice_bitcast_fusion.refs_0_), channel_id=1, source_target_pairs={{0,6},{1,7},{2,4},{3,5},{4,2},{5,3},{6,0},{7,1},{8,14},{9,15},{10,... | collective-permute-start | bytes 1769480 | tf_op jit(solution)/shard_map/ppermute | solution.py:1028
  541.8 30.9 %collective-permute-start.52 = (bf16[384,768]{1,0:T(8,128)(2,1)}, bf16[384,768]{1,0:T(8,128)(2,1)}, u32[]{:S(2)}, u32[]{:S(2)}) collective-permute-start(bf16[384,768]{1,0:T(8,128)(2,1)} %dynamic-slice_bitcast_fusion.refs_0_), channel_id=1, source_target_pairs={{0,8},{1,9},{2,10},{3,11},{4,12},{5,13},{6,14},{7,15},{8,0},{9,1},... | collective-permute-start | bytes 1769480 | tf_op jit(solution)/shard_map/ppermute | solution.py:1028
  (88 other events, 1152.1 us)
Sparse Core Ops, SparseCore 0:
  88.7 57.0 all-gather.2
  383.7 40.2 reduce-scatter.1
  457.8 32.8 all-gather.4
